TPU v7x, 32 devices: a whole 2x2x4 slice. The times are simulated.
32 devices in a mesh: batch: 4 (over y, x), seq: 8 (over z, core).
Axes of the slice: x: 2, y: 2, z: 4, core: 2. Of those that a mesh axis runs over, the one named last changes fastest.
Arguments:
- inputs: bfloat16 [8, 1024, 512], P('batch', 'seq'), may hold values from -6 to 6
- doc_starts: int32 [8, 4], P('batch'), may hold values from 0 to 1023, as said below
- cotangent: bfloat16 [8, 1024, 512], P('batch', 'seq'), may hold values from -6 to 6
- norm_gain: bfloat16 [2, 2, 512], replicated, may hold values from 0.099609375 to 1.8984375
- norm_bias: bfloat16 [2, 2, 512], replicated, may hold values from -1 to 1
- qkv_weight: bfloat16 [2, 512, 1536], replicated, may hold values from -0.25 to 0.25
- qkv_bias: bfloat16 [2, 3, 512], replicated, may hold values from -1 to 1
- out_weight: bfloat16 [2, 512, 512], replicated, may hold values from -1 to 1
- out_bias: bfloat16 [2, 512], replicated, may hold values from -1 to 1
- in_weight: bfloat16 [2, 512, 2048], replicated, may hold values from -0.25 to 0.25
- in_bias: bfloat16 [2, 2048], replicated, may hold values from -1.5 to 1.5
- down_weight: bfloat16 [2, 2048, 512], replicated, may hold values from -0.125 to 0.125
- down_bias: bfloat16 [2, 512], replicated, may hold values from -1 to 1
Outputs:
- result: bfloat16 [8, 1024, 512], P('batch', 'seq')
- grad_inputs: float32 [8, 1024, 512], P('batch', 'seq')
- grad_norm_gain: float32 [2, 2, 512], P(None, None, 'seq')
- grad_norm_bias: float32 [2, 2, 512], P(None, None, 'seq')
- grad_qkv_weight: float32 [2, 512, 1536], P(None, 'seq')
- grad_qkv_bias: float32 [2, 3, 512], P(None, None, 'seq')
- grad_out_weight: float32 [2, 512, 512], P(None, 'seq')
- grad_out_bias: float32 [2, 512], P(None, 'seq')
- grad_in_weight: float32 [2, 512, 2048], P(None, 'seq')
- grad_in_bias: float32 [2, 2048], P(None, 'seq')
- grad_down_weight: float32 [2, 2048, 512], P(None, 'seq')
- grad_down_bias: float32 [2, 512], P(None, 'seq')
Inputs may be any that keep to these rules, and one draw needn't show every extreme that they name: `doc_starts`: in each row the entries are nondecreasing and the first is 0; an entry p > 0 marks the first token of a document at place p of the row, and repeated entries mark one start. In each aligned block of 2 rows that share an index of batch, at least one row holds only zeros.
All inputs are finite; a program needn't handle non-finite values.
Results may differ from a plain program's by a relative error of at most 0.008.
Values sent between devices are 32-bit elements; how exact they have to be, the bound alone decides.
No kernel may reach another device: no remote copies, remote signals or barrier semaphores. Data moves between devices by JAX's collectives and lax.ppermute only.
A program may use at most 192 MiB of HBM per device.

v0:
```python
import math

import jax
import jax.numpy as jnp
from jax import lax
from jax.sharding import PartitionSpec as P

D = 512
HEADS = 8
HEAD = 64
FEAT = 64
ROT = 16
GROUP = 64
LAYERS = 2


epsilon = 1e-05
PRECISE = lax.Precision.HIGHEST


def entering(value, axis, combine, identity, reverse):
    size, index = (lax.axis_size(axis), lax.axis_index(axis))
    everything = jax.tree.map(lambda part: lax.all_gather(part, axis), value)
    start = jax.tree.map(
        lambda part, zero: jnp.broadcast_to(jnp.asarray(zero, part.dtype), part.shape),
        value,
        identity,
    )

    def step(k, before):
        at = size - 1 - k if reverse else k
        reached = at > index if reverse else at < index
        new = combine(before, jax.tree.map(lambda part: part[at], everything))
        return jax.tree.map(lambda a, b: jnp.where(reached, a, b), new, before)

    return lax.fori_loop(0, size, step, start)


def cosine_table():
    frequency = jnp.arange(FEAT, dtype=jnp.float32)[:, None]
    columns = jnp.arange(HEAD, dtype=jnp.float32)[None, :]
    entries = jnp.cos(math.pi * (2.0 * columns + 1.0) * frequency / (2.0 * HEAD)) * math.sqrt(
        2.0 / HEAD
    )
    first_row = jnp.where(jnp.arange(FEAT) == 0, math.sqrt(0.5), 1.0)
    return entries * first_row[:, None]


def rotate(heads_x, places):
    half_rot = ROT // 2
    inverse = 10000.0 ** (-(jnp.arange(half_rot, dtype=jnp.float32) * 2.0 / ROT))
    angles = places.astype(jnp.float32)[..., None, None] * inverse
    cosine = jnp.cos(angles)
    sine_part = jnp.sin(angles)
    leading = heads_x[..., :half_rot]
    trailing = heads_x[..., half_rot:ROT]
    return jnp.concatenate(
        [
            leading * cosine - trailing * sine_part,
            trailing * cosine + leading * sine_part,
            heads_x[..., ROT:],
        ],
        axis=-1,
    )


def layer_norm(values, gain, shift):
    centred = values - jnp.mean(values, axis=-1, keepdims=True)
    variance = jnp.mean(centred * centred, axis=-1, keepdims=True)
    return centred * lax.rsqrt(variance + epsilon) * gain + shift


def exact_gelu(values):
    return jax.nn.gelu(values, approximate=False)


def combine_states(earlier, later):
    passing = 1.0 - later[2]
    return (
        later[0] + passing[:, None, None, None] * earlier[0],
        later[1] + passing[:, None, None] * earlier[1],
        jnp.maximum(earlier[2], later[2]),
    )


def per_device(
    inputs,
    doc_starts,
    cotangent,
    norm_gain,
    norm_bias,
    qkv_weight,
    qkv_bias,
    out_weight,
    out_bias,
    in_weight,
    in_bias,
    down_weight,
    down_bias,
):
    row_count = inputs.shape[0]
    length = inputs.shape[1]
    block_count = length // GROUP
    cosines = cosine_table()
    device_start = lax.axis_index("seq") * length
    absolute = device_start + jnp.arange(length, dtype=jnp.int32)
    segment = jnp.max(
        jnp.where(doc_starts[:, None, :] <= absolute[None, :, None], doc_starts[:, None, :], 0),
        axis=2,
    )
    places = absolute[None, :] - segment
    block_seg = segment.reshape(row_count, block_count, GROUP)
    positions = jnp.arange(GROUP)
    intra_mask = (
        (positions[None, :] <= positions[:, None])[None, None]
        & (block_seg[:, :, None, :] == block_seg[:, :, :, None])
    ).astype(jnp.float32)
    block_edges = device_start + GROUP * jnp.arange(block_count + 1, dtype=jnp.int32)
    cross_mask = (block_seg < block_edges[None, :block_count, None]).astype(jnp.float32)
    last_seg = block_seg[:, :, GROUP - 1]
    within = (absolute[None, None, :] < block_edges[None, 1:, None]) & (
        absolute[None, None, :] >= last_seg[:, :, None]
    )
    spread = jnp.concatenate(
        [jnp.zeros((row_count, 1, length), jnp.float32), within.astype(jnp.float32)], axis=1
    )
    spread_low = spread.astype(jnp.bfloat16)
    carry_keep = jnp.concatenate(
        [jnp.ones((row_count, 1), jnp.float32), (last_seg < device_start).astype(jnp.float32)],
        axis=1,
    )
    reset_flag = 1.0 - carry_keep[:, block_count]
    head_shape = (row_count, length, HEADS, HEAD)
    block_shape = (row_count, block_count, GROUP, HEADS)

    def featurize(heads_x):
        return jnp.exp(
            jnp.einsum("bthj,fj->bthf", rotate(heads_x, places), cosines, precision=PRECISE)
        )

    hidden = inputs.astype(jnp.float32)
    kept = []
    for depth_index in range(LAYERS):
        gains = norm_gain[depth_index].astype(jnp.float32)
        shifts = norm_bias[depth_index].astype(jnp.float32)
        first, first_back = jax.vjp(layer_norm, hidden, gains[0], shifts[0])
        second, second_back = jax.vjp(layer_norm, hidden, gains[1], shifts[1])
        first_low = first.astype(jnp.bfloat16)
        second_low = second.astype(jnp.bfloat16)
        packed = jnp.einsum(
            "btd,de->bte", first_low, qkv_weight[depth_index], preferred_element_type=jnp.float32
        ) + qkv_bias[depth_index].astype(jnp.float32).reshape(3 * D)
        query_feat, query_back = jax.vjp(featurize, packed[..., :D].reshape(head_shape))
        key_feat, key_back = jax.vjp(featurize, packed[..., D : 2 * D].reshape(head_shape))
        feat_query = query_feat.astype(jnp.bfloat16)
        feat_key = key_feat.astype(jnp.bfloat16)
        value_rows = packed[..., 2 * D :].reshape(head_shape).astype(jnp.bfloat16)
        keyed = spread_low[:, :, :, None, None] * feat_key[:, None]
        valued = spread_low[:, :, :, None, None] * value_rows[:, None]
        local_state = jnp.einsum(
            "bcshf,bshd->bchfd", keyed, value_rows, preferred_element_type=jnp.float32
        )
        local_norm = jnp.sum(keyed, axis=2, dtype=jnp.float32)
        zero_state = jnp.zeros_like(local_state[:, block_count])
        zero_norm = jnp.zeros_like(local_norm[:, block_count])
        carry_state, carry_norm, carry_flag = entering(
            (local_state[:, block_count], local_norm[:, block_count], reset_flag),
            "seq",
            combine_states,
            (zero_state, zero_norm, jnp.zeros_like(reset_flag)),
            False,
        )
        state_in = (
            local_state[:, :block_count]
            + carry_keep[:, :block_count, None, None, None] * carry_state[:, None]
        )
        norm_in = (
            local_norm[:, :block_count]
            + carry_keep[:, :block_count, None, None] * carry_norm[:, None]
        )
        query_blocks = feat_query.reshape(block_shape + (FEAT,))
        key_blocks = feat_key.reshape(block_shape + (FEAT,))
        value_blocks = value_rows.reshape(block_shape + (HEAD,))
        query_wide = query_blocks.astype(jnp.float32)
        scores = (
            jnp.einsum(
                "bcihf,bcjhf->bchij", query_blocks, key_blocks, preferred_element_type=jnp.float32
            )
            * intra_mask[:, :, None]
        )
        scores_low = scores.astype(jnp.bfloat16)
        numerator = jnp.einsum(
            "bchij,bcjhd->bcihd", scores_low, value_blocks, preferred_element_type=jnp.float32
        ) + cross_mask[..., None, None] * jnp.einsum(
            "bcihf,bchfd->bcihd", query_wide, state_in, precision=PRECISE
        )
        denominator = jnp.swapaxes(jnp.sum(scores, axis=-1), 2, 3) + cross_mask[
            ..., None
        ] * jnp.einsum("bcihf,bchf->bcih", query_wide, norm_in, precision=PRECISE)
        attended = numerator / denominator[..., None]
        attended_low = attended.reshape(row_count, length, D).astype(jnp.bfloat16)
        attn_out = jnp.einsum(
            "btd,de->bte", attended_low, out_weight[depth_index], preferred_element_type=jnp.float32
        ) + out_bias[depth_index].astype(jnp.float32)
        lifted = jnp.einsum(
            "btd,df->btf", second_low, in_weight[depth_index], preferred_element_type=jnp.float32
        ) + in_bias[depth_index].astype(jnp.float32)
        activated, gelu_back = jax.vjp(exact_gelu, lifted)
        act_low = activated.astype(jnp.bfloat16)
        feed = jnp.einsum(
            "btf,fd->btd", act_low, down_weight[depth_index], preferred_element_type=jnp.float32
        ) + down_bias[depth_index].astype(jnp.float32)
        kept.append(
            (
                first_back,
                second_back,
                first_low,
                second_low,
                query_back,
                key_back,
                query_blocks,
                key_blocks,
                value_blocks,
                query_wide,
                keyed,
                valued,
                state_in,
                norm_in,
                scores_low,
                denominator,
                attended,
                attended_low,
                gelu_back,
                act_low,
            )
        )
        hidden = hidden + attn_out + feed
    result = hidden.astype(jnp.bfloat16)
    upstream = cotangent.astype(jnp.float32)
    per_depth = [None] * LAYERS
    for depth_index in reversed(range(LAYERS)):
        (
            first_back,
            second_back,
            first_low,
            second_low,
            query_back,
            key_back,
            query_blocks,
            key_blocks,
            value_blocks,
            query_wide,
            keyed,
            valued,
            state_in,
            norm_in,
            scores_low,
            denominator,
            attended,
            attended_low,
            gelu_back,
            act_low,
        ) = kept[depth_index]
        upstream_low = upstream.astype(jnp.bfloat16)
        branch_bias = jnp.sum(upstream_low, axis=(0, 1), dtype=jnp.float32)
        grad_down = jnp.einsum(
            "btf,btd->fd", act_low, upstream_low, preferred_element_type=jnp.float32
        )
        grad_lift = gelu_back(
            jnp.einsum(
                "btd,fd->btf",
                upstream_low,
                down_weight[depth_index],
                preferred_element_type=jnp.float32,
            )
        )[0].astype(jnp.bfloat16)
        grad_in_b = jnp.sum(grad_lift, axis=(0, 1), dtype=jnp.float32)
        grad_in = jnp.einsum(
            "btd,btf->df", second_low, grad_lift, preferred_element_type=jnp.float32
        )
        grad_second = jnp.einsum(
            "btf,df->btd", grad_lift, in_weight[depth_index], preferred_element_type=jnp.float32
        )
        grad_out = jnp.einsum(
            "btd,bte->de", attended_low, upstream_low, preferred_element_type=jnp.float32
        )
        grad_attended = jnp.einsum(
            "bte,de->btd", upstream_low, out_weight[depth_index], preferred_element_type=jnp.float32
        ).reshape(attended.shape)
        grad_num = (grad_attended / denominator[..., None]).astype(jnp.bfloat16)
        grad_den = -jnp.sum(grad_attended * attended, axis=-1) / denominator
        grad_scores = (
            (
                jnp.einsum(
                    "bcihd,bcjhd->bchij", grad_num, value_blocks, preferred_element_type=jnp.float32
                )
                + jnp.swapaxes(grad_den, 2, 3)[..., None]
            )
            * intra_mask[:, :, None]
        ).astype(jnp.bfloat16)
        num_wide = grad_num.astype(jnp.float32)
        grad_fq = jnp.einsum(
            "bchij,bcjhf->bcihf", grad_scores, key_blocks, preferred_element_type=jnp.float32
        ) + cross_mask[..., None, None] * (
            jnp.einsum("bcihd,bchfd->bcihf", num_wide, state_in, precision=PRECISE)
            + grad_den[..., None] * norm_in[:, :, None]
        )
        grad_fk = jnp.einsum(
            "bchij,bcihf->bcjhf", grad_scores, query_blocks, preferred_element_type=jnp.float32
        )
        grad_val = jnp.einsum(
            "bchij,bcihd->bcjhd", scores_low, grad_num, preferred_element_type=jnp.float32
        )
        cross_num = grad_num * cross_mask[..., None, None].astype(jnp.bfloat16)
        block_state = jnp.einsum(
            "bcihf,bcihd->bchfd", query_blocks, cross_num, preferred_element_type=jnp.float32
        )
        block_norm = jnp.einsum(
            "bcihf,bcih->bchf", query_wide, grad_den * cross_mask[..., None], precision=PRECISE
        )
        owed_state = jnp.sum(carry_keep[:, :block_count, None, None, None] * block_state, axis=1)
        owed_norm = jnp.sum(carry_keep[:, :block_count, None, None] * block_norm, axis=1)
        later_state, later_norm, later_flag = entering(
            (owed_state, owed_norm, reset_flag),
            "seq",
            combine_states,
            (jnp.zeros_like(owed_state), jnp.zeros_like(owed_norm), jnp.zeros_like(reset_flag)),
            True,
        )
        every_state = jnp.concatenate([block_state, later_state[:, None]], axis=1)
        every_norm = jnp.concatenate([block_norm, later_norm[:, None]], axis=1)
        grad_fk = (
            grad_fk.reshape(row_count, length, HEADS, FEAT)
            + jnp.einsum(
                "bcshd,bchfd->bshf", valued.astype(jnp.float32), every_state, precision=PRECISE
            )
            + jnp.einsum("bcs,bchf->bshf", spread, every_norm, precision=PRECISE)
        )
        grad_val = grad_val.reshape(head_shape) + jnp.einsum(
            "bcshf,bchfd->bshd", keyed.astype(jnp.float32), every_state, precision=PRECISE
        )
        grad_query = query_back(grad_fq.reshape(row_count, length, HEADS, FEAT))[0]
        grad_key = key_back(grad_fk)[0]
        grad_packed = jnp.concatenate(
            [
                grad_query.reshape(row_count, length, D),
                grad_key.reshape(row_count, length, D),
                grad_val.reshape(row_count, length, D),
            ],
            axis=-1,
        ).astype(jnp.bfloat16)
        grad_qkv_b = jnp.sum(grad_packed, axis=(0, 1), dtype=jnp.float32).reshape(3, D)
        grad_qkv = jnp.einsum(
            "btd,bte->de", first_low, grad_packed, preferred_element_type=jnp.float32
        )
        grad_first = jnp.einsum(
            "bte,de->btd", grad_packed, qkv_weight[depth_index], preferred_element_type=jnp.float32
        )
        input_first, gain_first, shift_first = first_back(grad_first)
        input_second, gain_second, shift_second = second_back(grad_second)
        upstream = upstream + input_first + input_second
        per_depth[depth_index] = (
            jnp.stack([gain_first, gain_second]),
            jnp.stack([shift_first, shift_second]),
            grad_qkv,
            grad_qkv_b,
            grad_out,
            branch_bias,
            grad_in,
            grad_in_b,
            grad_down,
            branch_bias,
        )
    stacked = [
        jnp.stack([per_depth[depth_index][member_index] for depth_index in range(LAYERS)])
        for member_index in range(10)
    ]
    (
        sum_gain,
        sum_shift,
        sum_qkv,
        sum_qkv_b,
        sum_out,
        sum_out_b,
        sum_in,
        sum_in_b,
        sum_down,
        sum_down_b,
    ) = stacked
    row_parts = (
        lax.psum_scatter(sum_gain, "seq", scatter_dimension=2, tiled=True),
        lax.psum_scatter(sum_shift, "seq", scatter_dimension=2, tiled=True),
        lax.psum_scatter(sum_qkv, "seq", scatter_dimension=1, tiled=True),
        lax.psum_scatter(sum_qkv_b, "seq", scatter_dimension=2, tiled=True),
        lax.psum_scatter(sum_out, "seq", scatter_dimension=1, tiled=True),
        lax.psum_scatter(sum_out_b, "seq", scatter_dimension=1, tiled=True),
        lax.psum_scatter(sum_in, "seq", scatter_dimension=1, tiled=True),
        lax.psum_scatter(sum_in_b, "seq", scatter_dimension=1, tiled=True),
        lax.psum_scatter(sum_down, "seq", scatter_dimension=1, tiled=True),
        lax.psum_scatter(sum_down_b, "seq", scatter_dimension=1, tiled=True),
    )
    summed = lax.psum(
        (
            row_parts[0],
            row_parts[1],
            row_parts[2],
            row_parts[3],
            row_parts[4],
            row_parts[5],
            row_parts[6],
            row_parts[7],
            row_parts[8],
            row_parts[9],
        ),
        "batch",
    )
    return (
        result,
        upstream,
        summed[0],
        summed[1],
        summed[2],
        summed[3],
        summed[4],
        summed[5],
        summed[6],
        summed[7],
        summed[8],
        summed[9],
    )


def solution(mesh):
    placed = (
        P("batch", "seq", None),
        P("batch", None),
        P("batch", "seq", None),
        P(),
        P(),
        P(),
        P(),
        P(),
        P(),
        P(),
        P(),
        P(),
        P(),
    )
    return jax.shard_map(
        per_device,
        mesh=mesh,
        in_specs=placed,
        out_specs=(
            P("batch", "seq", None),
            P("batch", "seq", None),
            P(None, None, "seq"),
            P(None, None, "seq"),
            P(None, "seq", None),
            P(None, None, "seq"),
            P(None, "seq", None),
            P(None, "seq"),
            P(None, "seq", None),
            P(None, "seq"),
            P(None, "seq", None),
            P(None, "seq"),
        ),
        check_vma=False,
    )
```

profile of v0, /device:TPU:0, one launch (start us, length us, event | category | flops | bytes accessed | tf_op | source)
XLA Modules:
  0.0 869.8 jit_solution(18403188765437852011)
XLA Ops:
  28.5 18.7 %all-reduce.14 = f32[16]{0:T(128)S(1)} all-reduce(f32[16]{0:T(128)S(1)} %dynamic-update-slice), channel_id=3, replica_groups=mesh['batch'=4,'seq'=8] {'seq'}, use_global_device_ids=true, to_apply=%add.14 | all-reduce | flops 16 | bytes 128
  49.7 14.6 %all-gather.2 = f32[16,1,8,64]{3,2,1,0:T(8,128)S(1)} all-gather(f32[2,1,8,64]{3,2,1,0:T(8,128)S(1)} %bitcast.554), channel_id=4, replica_groups=mesh['batch'=4,'seq'=8] {'seq'}, dimensions={0}, use_global_device_ids=true | all-gather | bytes 36864 | tf_op jit(solution)/shard_map/all_gather | solution.py:23
  68.0 2.9 fusion.211
  72.2 5.7 multiply_convert_fusion.1
  77.9 15.8 %while.68 = (s32[]{:T(128)}, f32[2,8,64,64]{3,2,1,0:T(8,128)S(1)}, f32[2,8,64]{2,1,0:T(8,128)S(1)}, s32[]{:T(128)}, f32[8,2,8,64,64]{4,3,2,1,0:T(8,128)}, /*inde...) while((s32[]{:T(128)}, f32[2,8,64,64]{3,2,1,0:T(8,128)S(1)}, ...), condition=%wide.region_5.6_spmd.clone, body=%wide.region_4.5_spmd.clone.sunk | while | flops 266246 | bytes 798887 | solution.py:36
  97.2 3.4 fusion.351
  120.5 14.1 %all-gather.4 = f32[16,1,8,64]{3,2,1,0:T(8,128)S(1)} all-gather(f32[2,1,8,64]{3,2,1,0:T(8,128)S(1)} %bitcast.555), channel_id=6, replica_groups=mesh['batch'=4,'seq'=8] {'seq'}, dimensions={0}, use_global_device_ids=true | all-gather | bytes 36864 | tf_op jit(solution)/shard_map/all_gather | solution.py:23
  138.0 5.1 fusion.212
  143.1 14.3 %all-gather.16.cloned.1.call-done = f32[16,1,8,64,64]{4,3,2,1,0:T(8,128)} async-done(((f32[2,1,8,64,64]{4,3,2,1,0:T(8,128)}), f32[16,1,8,64,64]{4,3,2,1,0:T(8,128)}) %all-gather.16.cloned.1.call-update) | async-done | bytes 2097168 | tf_op jit(solution)/shard_map/all_gather | solution.py:23
  157.4 15.7 %while.69 = (s32[]{:T(128)}, f32[2,8,64,64]{3,2,1,0:T(8,128)S(1)}, f32[2,8,64]{2,1,0:T(8,128)S(1)}, s32[]{:T(128)}, f32[8,2,8,64,64]{4,3,2,1,0:T(8,128)}, /*inde...) while((s32[]{:T(128)}, f32[2,8,64,64]{3,2,1,0:T(8,128)S(1)}, ...), condition=%wide.region_11.12_spmd.clone, body=%wide.region_10.11_spmd.clone.sunk | while | flops 266246 | bytes 798887 | solution.py:36
  186.2 7.4 multiply_convert_fusion
  193.6 3.7 convert_reduce_fusion
  222.8 14.0 %all-gather.6 = f32[16,8,64]{2,1,0:T(8,128)S(1)} all-gather(f32[2,8,64]{2,1,0:T(8,128)S(1)} %multiply_reduce_fusion.10), channel_id=8, replica_groups=mesh['batch'=4,'seq'=8] {'seq'}, dimensions={0}, use_global_device_ids=true | all-gather | bytes 36864 | tf_op jit(solution)/shard_map/all_gather | solution.py:23
  236.8 16.0 %while.70 = (s32[]{:T(128)}, f32[2,8,64,64]{3,2,1,0:T(8,128)S(1)}, f32[2,8,64]{2,1,0:T(8,128)S(1)}, s32[]{:T(128)}, f32[8,2,8,64,64]{4,3,2,1,0:T(8,128)}, /*inde...) while((s32[]{:T(128)}, f32[2,8,64,64]{3,2,1,0:T(8,128)S(1)}, ...), condition=%wide.region_17.18_spmd.clone, body=%wide.region_16.17_spmd.clone.sunk | while | flops 266250 | bytes 798949 | solution.py:36
  262.8 2.8 multiply_reduce_fusion.7
  303.3 14.4 %all-gather.8 = f32[16,8,64]{2,1,0:T(8,128)S(1)} all-gather(f32[2,8,64]{2,1,0:T(8,128)S(1)} %multiply_reduce_fusion.9), channel_id=10, replica_groups=mesh['batch'=4,'seq'=8] {'seq'}, dimensions={0}, use_global_device_ids=true | all-gather | bytes 36864 | tf_op jit(solution)/shard_map/all_gather | solution.py:23
  323.4 15.9 %while.71 = (s32[]{:T(128)}, f32[2,8,64,64]{3,2,1,0:T(8,128)S(1)}, f32[2,8,64]{2,1,0:T(8,128)S(1)}, s32[]{:T(128)}, f32[8,2,8,64,64]{4,3,2,1,0:T(8,128)}, /*inde...) while((s32[]{:T(128)}, f32[2,8,64,64]{3,2,1,0:T(8,128)S(1)}, ...), condition=%wide.region_26.27_spmd.clone, body=%wide.region_25.26_spmd.clone.sunk | while | flops 266250 | bytes 798949 | solution.py:36
  348.0 3.1 pad_maximum_fusion.2
  354.6 2.9 convert_reduce_fusion.1
  358.6 3.9 pad_maximum_fusion
  365.7 4.3 pad_maximum_fusion.1
  385.5 44.3 %reduce-scatter.20.cloned.1.call-done = f32[2,64,1536]{2,1,0:T(8,128)} async-done(((f32[2,512,1536]{2,1,0:T(8,128)}), f32[2,64,1536]{2,1,0:T(8,128)}) %reduce-scatter.20.cloned.1.call-update) | async-done | bytes 786448 | tf_op jit(solution)/shard_map/reduce_scatter | solution.py:393
  429.7 90.3 %reduce-scatter.24.cloned.1.call-done = f32[2,64,2048]{2,1,0:T(8,128)} async-done(((f32[2,512,2048]{2,1,0:T(8,128)}), f32[2,64,2048]{2,1,0:T(8,128)}) %reduce-scatter.24.cloned.1.call-update) | async-done | bytes 1048592 | tf_op jit(solution)/shard_map/reduce_scatter | solution.py:397
  520.0 90.3 %reduce-scatter.26.cloned.1.call-done = f32[2,256,512]{2,1,0:T(8,128)} async-done(((f32[2,2048,512]{2,1,0:T(8,128)}), f32[2,256,512]{2,1,0:T(8,128)}) %reduce-scatter.26.cloned.1.call-update) | async-done | bytes 1048592 | tf_op jit(solution)/shard_map/reduce_scatter | solution.py:399
  611.0 3.1 fusion.140
  614.1 27.1 %reduce-scatter.34.cloned.1.call-done = f32[64,2]{1,0:T(8,128)} async-done(((f32[512,2]{1,0:T(8,128)}), f32[64,2]{1,0:T(8,128)}) %reduce-scatter.34.cloned.1.call-update) | async-done | bytes 528
  642.1 32.5 %reduce-scatter.36.cloned.1.call-done = f32[256,2]{1,0:T(8,128)} async-done(((f32[2048,2]{1,0:T(8,128)}), f32[256,2]{1,0:T(8,128)}) %reduce-scatter.36.cloned.1.call-update) | async-done | bytes 2064
  676.7 29.0 %reduce-scatter.28.cloned.1.call-done = f32[64,4]{1,0:T(8,128)} async-done(((f32[512,4]{1,0:T(8,128)}), f32[64,4]{1,0:T(8,128)}) %reduce-scatter.28.cloned.1.call-update) | async-done | bytes 1040
  706.6 29.7 %reduce-scatter.30.cloned.1.call-done = f32[64,4]{1,0:T(8,128)} async-done(((f32[512,4]{1,0:T(8,128)}), f32[64,4]{1,0:T(8,128)}) %reduce-scatter.30.cloned.1.call-update) | async-done | bytes 1040
  737.3 30.0 %reduce-scatter.32.cloned.1.call-done = f32[64,6]{1,0:T(8,128)} async-done(((f32[512,6]{1,0:T(8,128)}), f32[64,6]{1,0:T(8,128)}) %reduce-scatter.32.cloned.1.call-update) | async-done | bytes 1552
  768.2 16.8 %all-reduce.15 = (f32[2,2,64]{2,1,0:T(2,128)}, f32[2,2,64]{2,1,0:T(2,128)}, f32[2,3,64]{2,1,0:T(4,128)S(1)}, f32[2,64]{1,0:T(2,128)S(1)}, f32[2,256]{1,0:T(2,128)}) all-reduce(f32[2,2,64]{2,1,0:T(2,128)S(1)} %copy.503, f32[2,2,64]{2,1,0:T(2,128)S(1)} %copy.505, ...), channel_id=1, replica_groups=mesh['batch'=4,'seq'=8] {'batch'}, use_global_device_ids=true, to_apply=%region_36.37 | all-reduce | flops 1536 | bytes 12288 | tf_op jit(solution)/shard_map/psum | solution.py:402
  785.6 70.9 %all-reduce.19.cloned.1.call-done = (f32[2,64,1536]{2,1,0:T(8,128)}, f32[2,64,512]{2,1,0:T(8,128)}, f32[2,64,2048]{2,1,0:T(8,128)}, f32[2,256,512]{2,1,0:T(8,128)}) async-done(((f32[2,64,1536]{2,1,0:T(8,128)}, f32[2,64,512]{2,1,0:T(8,128)}, f32[2,64,2048]{2,1,0:T(8,128)}, f32[2,256,512]{2,1,0:T(8,128)}), (f32[2,64,1536]{2,1,0:T(8,128)}, f32[2,64,512]{2,1,0:T(8,128)}, f32[2,64,2048]{2,1,0:T(8,128)}, ...) | async-done | bytes 3145744 | tf_op jit(solution)/shard_map/psum | solution.py:402
  (680 shorter events, 252.0 us)
Async XLA Ops:
  7.2 70.8 %all-gather.14.cloned.1.call-start = ((), (), s32[]{:S(2)}) async-start(), calls=%async_computation.13 | async-start | bytes 4718592 | tf_op jit(solution)/shard_map/all_gather | solution.py:23
  9.2 58.7 %copy-start.97 = (f32[2,128]{1,0:T(2,128)}, f32[2,128]{1,0:T(2,128)S(1)}, u32[]{:S(2)}) copy-start(f32[2,128]{1,0:T(2,128)S(1)} %broadcast_multiply_fusion.3) | copy-start | bytes 3076
  12.7 55.2 %copy-start.93 = (f32[1,1,512]{2,1,0:T(1,128)}, f32[1,1,512]{2,1,0:T(1,128)S(1)}, u32[]{:S(2)}) copy-start(f32[1,1,512]{2,1,0:T(1,128)S(1)} %get-tuple-element.1005) | copy-start | bytes 6148
  12.7 254.1 %copy-start.89 = (f32[1,1,512]{2,1,0:T(1,128)}, f32[1,1,512]{2,1,0:T(1,128)S(1)}, u32[]{:S(2)}) copy-start(f32[1,1,512]{2,1,0:T(1,128)S(1)} %get-tuple-element.958) | copy-start | bytes 6148
  13.3 54.6 %copy-start.111 = (f32[1,1,512]{2,1,0:T(1,128)}, f32[1,1,512]{2,1,0:T(1,128)S(1)}, u32[]{:S(2)}) copy-start(f32[1,1,512]{2,1,0:T(1,128)S(1)} %get-tuple-element.1003) | copy-start | bytes 6148
  19.2 77.9 %copy-start.5 = (f32[2,3,8,64,64]{3,4,1,2,0:T(8,128)}, f32[2,3,8,64,64]{3,4,1,2,0:T(8,128)S(1)}, u32[]{:S(2)}) copy-start(f32[2,3,8,64,64]{3,4,1,2,0:T(8,128)S(1)} %convolution_bitcast_fusion.7) | copy-start | bytes 2359300
  22.3 135.1 %all-gather.16.cloned.1.call-start = ((), (), s32[]{:S(2)}) async-start(), calls=%async_computation.14 | async-start | bytes 4718592 | tf_op jit(solution)/shard_map/all_gather | solution.py:23
  22.4 41.9 %copy-start.141 = (bf16[2,512]{1,0:T(2,128)(2,1)S(1)}, bf16[2,512]{1,0:T(2,128)(2,1)}, u32[]{:S(2)}) copy-start(bf16[2,512]{1,0:T(2,128)(2,1)} %param.29) | copy-start | bytes 6148
  22.4 42.5 %copy-start.142 = (bf16[2,512]{1,0:T(2,128)(2,1)S(1)}, bf16[2,512]{1,0:T(2,128)(2,1)}, u32[]{:S(2)}) copy-start(bf16[2,512]{1,0:T(2,128)(2,1)} %param.33) | copy-start | bytes 6148
  26.9 40.4 %copy-start.45 = (bf16[2,2,64,8,64]{2,1,4,3,0:T(2,128)(2,1)}, bf16[2,2,64,8,64]{2,1,4,3,0:T(2,128)(2,1)S(1)}, u32[]{:S(2)}) copy-start(bf16[2,2,64,8,64]{2,1,4,3,0:T(2,128)(2,1)S(1)} %reshape.539) | copy-start | bytes 786436
  105.3 215.3 %copy-start.95 = (f32[2,128]{1,0:T(2,128)}, f32[2,128]{1,0:T(2,128)S(1)}, u32[]{:S(2)}) copy-start(f32[2,128]{1,0:T(2,128)S(1)} %broadcast_multiply_fusion.2) | copy-start | bytes 3076
  105.6 215.0 %copy-start.109 = (f32[2,128]{1,0:T(2,128)}, f32[2,128]{1,0:T(2,128)S(1)}, u32[]{:S(2)}) copy-start(f32[2,128]{1,0:T(2,128)S(1)} %fusion.312) | copy-start | bytes 3076
  111.7 125.1 %all-gather.18.cloned.1.call-start = ((), (), s32[]{:S(2)}) async-start(), calls=%async_computation.15 | async-start | bytes 4718592 | tf_op jit(solution)/shard_map/all_gather | solution.py:23
  119.3 56.1 %copy-start.11 = (bf16[2,2,64,8,64]{2,1,4,3,0:T(2,128)(2,1)}, bf16[2,2,64,8,64]{2,1,4,3,0:T(2,128)(2,1)S(1)}, u32[]{:S(2)}) copy-start(bf16[2,2,64,8,64]{2,1,4,3,0:T(2,128)(2,1)S(1)} %reshape.541) | copy-start | bytes 786436
  186.1 137.3 %all-gather.20.cloned.1.call-start = ((), (), s32[]{:S(2)}) async-start(), calls=%async_computation.16 | async-start | bytes 4718592 | tf_op jit(solution)/shard_map/all_gather | solution.py:23
  275.8 109.6 %reduce-scatter.22.cloned.1.call-start = ((), (), s32[]{:S(2)}) async-start(), calls=%async_computation.10 | async-start | bytes 2359296 | tf_op jit(solution)/shard_map/reduce_scatter | solution.py:395
  323.0 106.7 %reduce-scatter.20.cloned.1.call-start = ((), (), s32[]{:S(2)}) async-start(), calls=%async_computation.9 | async-start | bytes 7077888 | tf_op jit(solution)/shard_map/reduce_scatter | solution.py:393
  351.2 168.8 %reduce-scatter.24.cloned.1.call-start = ((), (), s32[]{:S(2)}) async-start(), calls=%async_computation.11 | async-start | bytes 9437184 | tf_op jit(solution)/shard_map/reduce_scatter | solution.py:397
  362.5 247.8 %reduce-scatter.26.cloned.1.call-start = ((), (), s32[]{:S(2)}) async-start(), calls=%async_computation.12 | async-start | bytes 9437184 | tf_op jit(solution)/shard_map/reduce_scatter | solution.py:399
  370.1 271.1 %reduce-scatter.34.cloned.1.call-start = ((), (), s32[]{:S(2)}) async-start(), calls=%async_computation.20 | async-start | bytes 294912
  371.7 302.8 %reduce-scatter.36.cloned.1.call-start = ((), (), s32[]{:S(2)}) async-start(), calls=%async_computation.21 | async-start | bytes 1179648
  373.3 332.4 %reduce-scatter.28.cloned.1.call-start = ((), (), s32[]{:S(2)}) async-start(), calls=%async_computation.17 | async-start | bytes 294912
  380.6 355.7 %reduce-scatter.30.cloned.1.call-start = ((), (), s32[]{:S(2)}) async-start(), calls=%async_computation.18 | async-start | bytes 294912
  382.1 385.2 %reduce-scatter.32.cloned.1.call-start = ((), (), s32[]{:S(2)}) async-start(), calls=%async_computation.19 | async-start | bytes 294912
  383.2 227.1 %copy-start.18 = (bf16[2,512,512]{2,1,0:T(8,128)(2,1)S(1)}, bf16[2,512,512]{2,1,0:T(8,128)(2,1)}, u32[]{:S(2)}) copy-start(bf16[2,512,512]{2,1,0:T(8,128)(2,1)} %param.28) | copy-start | bytes 3145732
  383.2 227.1 %copy-start.31 = (bf16[2,128,512]{2,1,0:T(8,128)(2,1)S(1)}, bf16[2,128,512]{2,1,0:T(8,128)(2,1)}, u32[]{:S(2)}) copy-start(bf16[2,128,512]{2,1,0:T(8,128)(2,1)} %convert_element_type.325) | copy-start | bytes 786436
  383.2 227.1 %copy-start.145 = (f32[1,512]{1,0:T(1,128)S(1)}, f32[1,512]{1,0:T(1,128)}, u32[]{:S(2)}) copy-start(f32[1,512]{1,0:T(1,128)} %get-tuple-element.972) | copy-start | bytes 6148
  385.4 471.1 %all-reduce.19.cloned.1.call-start = ((), (), s32[]{:S(2)}) async-start(), calls=%async_computation.22 | async-start | bytes 6291456 | tf_op jit(solution)/shard_map/psum | solution.py:402
  611.0 64.5 %copy-start.52 = (f32[2,128,512]{2,1,0:T(8,128)S(1)}, f32[2,128,512]{2,1,0:T(8,128)}, u32[]{:S(2)}) copy-start(f32[2,128,512]{2,1,0:T(8,128)} %copy-done.51) | copy-start | bytes 1572868
  611.0 64.6 %copy-start.58 = (f32[2,128,512]{2,1,0:T(8,128)S(1)}, f32[2,128,512]{2,1,0:T(8,128)}, u32[]{:S(2)}) copy-start(f32[2,128,512]{2,1,0:T(8,128)} %copy-done.57) | copy-start | bytes 1572868
  611.0 64.6 %copy-start.67 = (f32[2,128,512]{2,1,0:T(8,128)S(1)}, f32[2,128,512]{2,1,0:T(8,128)}, u32[]{:S(2)}) copy-start(f32[2,128,512]{2,1,0:T(8,128)} %get-tuple-element.903) | copy-start | bytes 1572868
  785.0 76.8 %copy-start.152 = (f32[2,64]{1,0:T(2,128)}, f32[2,64]{1,0:T(2,128)S(1)}, u32[]{:S(2)}) copy-start(f32[2,64]{1,0:T(2,128)S(1)} %get-tuple-element.1335) | copy-start | bytes 1540
  (140 other events, 607.7 us)
Sparse Core Ops, SparseCore 0:
  22.4 50.5 all-gather.13
  111.8 45.5 all-gather.15
  186.2 46.1 all-gather.17
  275.9 46.4 all-gather.19
  324.6 34.4 reduce-scatter.21
  361.2 68.4 reduce-scatter.19
  432.0 87.9 reduce-scatter.23
  522.3 87.9 reduce-scatter.25
  612.5 28.6 reduce-scatter.33
  644.0 30.4 reduce-scatter.35
  676.9 28.7 reduce-scatter.27
  707.7 28.5 reduce-scatter.29
  738.6 28.5 reduce-scatter.31
  770.5 85.9 all-reduce.18
where the time goes:
time: 880 us; the launch traced here: 870 us
  waiting for transfers between devices  458 us (52%)
  other arithmetic  113 us (13%)
  matrix products  96.5 us (11%)
  blocking collectives  92.5 us (11%)
  local copies, waits for them, and re-layouts  88.8 us (10%)
  between operations  17.5 us (2%)
    unnamed x19, waiting for transfers between devices  149 us
    reduce_scatter x1, waiting for transfers between devices, per_device(): lax.psum_scatter(sum_down, 'seq', scatter_dimension=1, tiled=True)  90.3 us
    reduce_scatter x1, waiting for transfers between devices, per_device(): lax.psum_scatter(sum_in, 'seq', scatter_dimension=1, tiled=True)  90.3 us
    psum x1, waiting for transfers between devices, per_device(): lax.psum((row_parts[0], row_parts[1], row_parts[2], row_parts[3], row_par...  70.9 us
    all_gather x4, blocking collectives, entering(): everything = jax.tree.map(lambda part: lax.all_gather(part, axis), value)  57 us
    reduce_scatter x1, waiting for transfers between devices, per_device(): lax.psum_scatter(sum_qkv, 'seq', scatter_dimension=1, tiled=True)  44.3 us
    select_n x64, other arithmetic, step(): return jax.tree.map(lambda a, b: jnp.where(reached, a, b), new, before)  40 us
    unnamed x337, local copies, waits for them, and re-layouts  32.2 us
  transfers between devices with their start and end apart: 14, of which 10 were waited for; matrix products, arithmetic and copies ran while one was open for 19% of the time, Pallas kernels for 0%

commit v1 on v0

v1 whole, which is shorter than its diff:
```python
import functools
import math

import jax
import jax.numpy as jnp
import numpy as np
from jax import lax
from jax.experimental import pallas as pl
from jax.experimental.pallas import tpu as pltpu
from jax.sharding import PartitionSpec as P

D = 512
HEADS = 8
HEAD = 64
FF = 2048
ROT = 16
LAYERS = 2
NDOC = 4
LEN = 128
PAIRS = HEADS // 2
PACK = 2 * HEAD + 8
WIDE = 512

epsilon = 1e-05
f32, bf16 = jnp.float32, jnp.bfloat16
NN = (((1,), (0,)), ((), ()))
NT = (((1,), (1,)), ((), ()))
TN = (((0,), (0,)), ((), ()))


def dot(a, b, dims=NN):
    return lax.dot_general(a, b, dims, preferred_element_type=f32)


def split(x):
    high = x.astype(bf16)
    return high, (x - high.astype(f32)).astype(bf16)


def sds(shape, dtype=f32):
    return jax.ShapeDtypeStruct(shape, dtype)


def norm_parts(hidden):
    centred = hidden - jnp.mean(hidden, axis=-1, keepdims=True)
    variance = jnp.mean(centred * centred, axis=-1, keepdims=True)
    inverse = lax.rsqrt(variance + epsilon)
    return centred * inverse, inverse


def segment_of(position, starts, row):
    found = jnp.zeros_like(position)
    for k in range(NDOC):
        entry = starts[row, k]
        found = jnp.maximum(found, jnp.where(entry <= position, entry, 0))
    return found


def masks_of(row, meta, starts):
    begin = meta[0]
    at_i = begin + lax.broadcasted_iota(jnp.int32, (LEN, 128), 0)
    at_j = begin + lax.broadcasted_iota(jnp.int32, (LEN, 128), 1)
    seg_i, seg_j = segment_of(at_i, starts, row), segment_of(at_j, starts, row)
    last = jnp.int32(0)
    for k in range(NDOC):
        entry = starts[row, k]
        last = jnp.maximum(last, jnp.where(entry <= begin + (LEN - 1), entry, 0))
    intra = jnp.where((at_j <= at_i) & (seg_i == seg_j), 1.0, 0.0).astype(f32)
    cross = jnp.where(seg_i < begin, 1.0, 0.0).astype(f32)
    tail = jnp.where(seg_i == last, 1.0, 0.0).astype(f32)
    return intra, cross, tail


def low_lanes(rows):
    return lax.broadcasted_iota(jnp.int32, (rows, 128), 1) < HEAD


def rotate(x, tables):
    base, ahead, behind = tables
    return x * base + pltpu.roll(x, 120, 1) * ahead + pltpu.roll(x, 8, 1) * behind


def rotate_back(g, tables):
    base, ahead, behind = tables
    return g * base + pltpu.roll(g * ahead, 8, 1) + pltpu.roll(g * behind, 120, 1)


def featurize(x, tables, high, low):
    pieces = [rotate(x[:, g * 128 : (g + 1) * 128], tables) for g in range(4)]
    found = []
    for g in range(2):
        a, b = split(jnp.concatenate(pieces[2 * g : 2 * g + 2], axis=1))
        found.append(jnp.exp(dot(a, high) + dot(b, high) + dot(a, low)))
    return jnp.concatenate(found, axis=1)


def unfeaturize(g, tables, high, low):
    found = []
    for k in range(2):
        a, b = split(g[:, k * 256 : (k + 1) * 256])
        back = dot(a, high, NT) + dot(b, high, NT) + dot(a, low, NT)
        found += [rotate_back(back[:, :128], tables), rotate_back(back[:, 128:], tables)]
    return jnp.concatenate(found, axis=1)


def head_ones():
    across = lax.broadcasted_iota(jnp.int32, (256, 256), 0) // HEAD
    along = lax.broadcasted_iota(jnp.int32, (256, 256), 1) // HEAD
    return jnp.where(across == along, 1.0, 0.0).astype(bf16)


def head_sum(x, ones):
    found = []
    for g in range(2):
        a, b = split(x[:, g * 256 : (g + 1) * 256])
        found.append(dot(a, ones) + dot(b, ones))
    return jnp.concatenate(found, axis=1)


def store_halves(meta, keep_ref, send_ref, halves):
    def put(ref, half):
        for row, at, value in halves[half]:
            ref[row, at[0] : at[1], :] = value

    core = meta[1]
    for mine in range(2):

        @pl.when(core == mine)
        def _():
            put(keep_ref, mine)
            put(send_ref, 1 - mine)


def pack_states(rows, left_of, right, norm_of):
    low = low_lanes(HEAD)
    halves = [[], []]
    for row in range(rows):
        at = slice(row * LEN, (row + 1) * LEN)
        left, norm = left_of(row), norm_of(row)
        for pair in range(PAIRS):
            lanes = slice(pair * 128, (pair + 1) * 128)
            both = dot(left[:, lanes], right[at, lanes], TN)
            half, place = pair // 2, pair % 2
            halves[half].append(
                (row, (place * HEAD, (place + 1) * HEAD), jnp.where(low, both[:HEAD], both[HEAD:]))
            )
        for half in range(2):
            pieces = [norm[:, (2 * half + k) * 128 : (2 * half + k + 1) * 128] for k in range(2)]
            block = jnp.concatenate(pieces + [jnp.zeros((6, 128), f32)], axis=0)
            halves[half].append((row, (2 * HEAD, PACK), block))
    return halves


def unpack_state(meta, mine_ref, theirs_ref, row):
    low = low_lanes(HEAD)
    blocks, norms = [], []
    for half in range(2):
        packed = jnp.where(meta[1] == half, mine_ref[row], theirs_ref[row])
        for place in range(2):
            state = packed[place * HEAD : (place + 1) * HEAD]
            both = jnp.concatenate(
                [jnp.where(low, state, 0.0), jnp.where(low, 0.0, state)], axis=0
            )
            blocks.append(split(both))
            norms.append(packed[2 * HEAD + place : 2 * HEAD + place + 1])
    return blocks, jnp.concatenate(norms, axis=1)


def cross_dot(x, block, dims=NN):
    return dot(x, block[0], dims) + dot(x, block[1], dims)


def gelu_parts(lifted):
    phi = 0.5 + 0.5 * lax.erf(lifted * math.sqrt(0.5))
    slope = phi + lifted * (jnp.exp(-0.5 * lifted * lifted) * (1.0 / math.sqrt(2.0 * math.pi)))
    return lifted * phi, slope


def norm_back(grad, xhat, inverse, gain):
    u = grad * gain
    mean_u = jnp.mean(u, axis=-1, keepdims=True)
    mean_ux = jnp.mean(u * xhat, axis=-1, keepdims=True)
    down = (u - mean_u - xhat * mean_ux) * inverse
    return down, jnp.sum(grad * xhat, axis=0, keepdims=True), jnp.sum(grad, axis=0, keepdims=True)


def front_body(meta, starts, hidden, gain, shift, w, b, tables, dct, outs):
    first_ref, second_ref, fq_ref, fk_ref, v_ref, eq_ref, ek_ref, keep_ref, send_ref = outs
    xhat, _ = norm_parts(hidden)
    gains, shifts = gain[...].astype(f32), shift[...].astype(f32)
    first = (xhat * gains[0:1] + shifts[0:1]).astype(bf16)
    first_ref[...] = first
    second_ref[...] = (xhat * gains[1:2] + shifts[1:2]).astype(bf16)
    bias = b[...].astype(f32)
    tabs = tuple(t[...] for t in tables)
    high, low = dct[0][...], dct[1][...]
    keys = dot(first, w[:, D : 2 * D]) + bias[1:2]
    values = (dot(first, w[:, 2 * D :]) + bias[2:3]).astype(bf16)
    v_ref[...] = values
    exp_k = featurize(keys, tabs, high, low)
    ek_ref[...] = exp_k
    feat_k = exp_k.astype(bf16)
    fk_ref[...] = feat_k
    rows = hidden.shape[0] // LEN
    wide = feat_k.astype(f32)

    def tailed(row):
        tail = masks_of(row, meta, starts)[2]
        return wide[row * LEN : (row + 1) * LEN] * jnp.concatenate([tail] * 4, axis=1)

    kept = [tailed(row) for row in range(rows)]
    halves = pack_states(
        rows,
        lambda row: kept[row].astype(bf16),
        values,
        lambda row: jnp.sum(kept[row], axis=0, keepdims=True),
    )
    store_halves(meta, keep_ref, send_ref, halves)
    queries = dot(first, w[:, :D]) + bias[0:1]
    exp_q = featurize(queries, tabs, high, low)
    eq_ref[...] = exp_q
    fq_ref[...] = exp_q.astype(bf16)


def front_kernel(meta, starts, h, gain, shift, w, b, ta, tb, tc, dh, dl, *outs):
    front_body(meta, starts, h[...].astype(f32), gain, shift, w, b, (ta, tb, tc), (dh, dl), outs)


def attend(meta, starts, num_ref, kt_ref, fq_ref, mine_ref, theirs_ref, den_ref, att_ref, low_ref):
    rows = num_ref.shape[0] // LEN
    ones = head_ones()
    for row in range(rows):
        at = slice(row * LEN, (row + 1) * LEN)
        cross = masks_of(row, meta, starts)[1]
        cross4 = jnp.concatenate([cross] * 4, axis=1)
        blocks, norm = unpack_state(meta, mine_ref, theirs_ref, row)
        fq = fq_ref[at]
        far = jnp.concatenate(
            [cross_dot(fq[:, p * 128 : (p + 1) * 128], blocks[p]) for p in range(PAIRS)], axis=1
        )
        num = num_ref[at] + cross4 * far
        den = head_sum(fq.astype(f32) * (kt_ref[at] + cross4 * norm), ones)
        att = num / den
        den_ref[at] = den
        att_ref[at] = att
        low_ref[at] = att.astype(bf16)


def middle_kernel(
    meta, starts, h, feed, num, kt, fq0, mine, theirs, ow, ob, gain, shift, w, b, ta, tb, tc, dh, dl,
    den, att, att_low, h2, *outs,
):
    attend(meta, starts, num, kt, fq0, mine, theirs, den, att, att_low)
    hidden = h[...].astype(f32) + (dot(att_low[...], ow[...]) + ob[...].astype(f32)) + feed[...]
    h2[...] = hidden
    front_body(meta, starts, hidden, gain, shift, w, b, (ta, tb, tc), (dh, dl), outs)


def attend_back(meta, starts, up, ow, den, att, fq, gnum, gden, keep_ref, send_ref):
    ga = dot(up, ow[...], NT)
    den_v = den[...]
    gn = (ga / den_v).astype(bf16)
    gnum[...] = gn
    gd = -head_sum(ga * att[...], head_ones()) / den_v
    gden[...] = gd
    rows = up.shape[0] // LEN
    wide = fq[...].astype(f32)

    def crossed(row):
        cross = masks_of(row, meta, starts)[1]
        return wide[row * LEN : (row + 1) * LEN] * jnp.concatenate([cross] * 4, axis=1)

    kept = [crossed(row) for row in range(rows)]
    halves = pack_states(
        rows,
        lambda row: kept[row].astype(bf16),
        gn,
        lambda row: jnp.sum(kept[row] * gd[row * LEN : (row + 1) * LEN], axis=0, keepdims=True),
    )
    store_halves(meta, keep_ref, send_ref, halves)


def turn_kernel(
    meta, starts, h, feed, num, kt, fq, mine, theirs, ow, ob, cot,
    den, att, att_low, result, gnum, gden, keep, send, gob,
):
    attend(meta, starts, num, kt, fq, mine, theirs, den, att, att_low)
    attend_back(meta, starts, cot[...], ow, den, att, fq, gnum, gden, keep, send)
    hidden = h[...] + (dot(att_low[...], ow[...]) + ob[...].astype(f32)) + feed[...]
    result[...] = hidden.astype(bf16)
    gob[...] = jnp.sum(cot[...].astype(f32), axis=0, keepdims=True)


def feed_kernel(second, iw, ib, dw, db, act, slope, feed):
    total = jnp.broadcast_to(db[...].astype(f32), feed.shape)
    for g in range(FF // WIDE):
        lanes = slice(g * WIDE, (g + 1) * WIDE)
        lifted = dot(second[...], iw[:, lanes]) + ib[:, lanes].astype(f32)
        value, grad = gelu_parts(lifted)
        low = value.astype(bf16)
        act[:, lanes] = low
        slope[:, lanes] = grad
        total = total + dot(low, dw[lanes, :])
    feed[...] = total


def feed_back_kernel(slope, up, iw, dw, lift, gsecond, gib):
    total = jnp.zeros(gsecond.shape, f32)
    for g in range(FF // WIDE):
        lanes = slice(g * WIDE, (g + 1) * WIDE)
        low = (dot(up[...], dw[lanes, :], NT) * slope[:, lanes]).astype(bf16)
        lift[:, lanes] = low
        gib[:, lanes] = jnp.sum(low.astype(f32), axis=0, keepdims=True)
        total = total + dot(low, iw[:, lanes], NT)
    gsecond[...] = total


def feed_both_kernel(second, iw, ib, dw, db, up, act, feed, lift, gsecond, gib):
    total = jnp.broadcast_to(db[...].astype(f32), feed.shape)
    back = jnp.zeros(gsecond.shape, f32)
    for g in range(FF // WIDE):
        lanes = slice(g * WIDE, (g + 1) * WIDE)
        lifted = dot(second[...], iw[:, lanes]) + ib[:, lanes].astype(f32)
        value, grad = gelu_parts(lifted)
        low = value.astype(bf16)
        act[:, lanes] = low
        total = total + dot(low, dw[lanes, :])
        low = (dot(up[...], dw[lanes, :], NT) * grad).astype(bf16)
        lift[:, lanes] = low
        gib[:, lanes] = jnp.sum(low.astype(f32), axis=0, keepdims=True)
        back = back + dot(low, iw[:, lanes], NT)
    feed[...] = total
    gsecond[...] = back


def intra_kernel(meta, starts, fq, fk, v, scores, num, kt):
    low = low_lanes(LEN)
    even = jnp.where(low, 1.0, 0.0).astype(bf16)
    odd = jnp.where(low, 0.0, 1.0).astype(bf16)
    for row in range(fq.shape[0] // LEN):
        at = slice(row * LEN, (row + 1) * LEN)
        intra = masks_of(row, meta, starts)[0]
        kt[at] = dot(intra.astype(bf16), fk[at])
        twice = jnp.concatenate([intra, intra], axis=0)
        for pair in range(PAIRS):
            lanes = slice(pair * 128, (pair + 1) * 128)
            q = fq[at, lanes]
            both = jnp.concatenate([q * even, q * odd], axis=0)
            rounded = (dot(both, fk[at, lanes], NT) * twice).astype(bf16)
            scores[row, pair] = rounded
            out = dot(rounded, v[at, lanes])
            num[at, lanes] = jnp.where(low, out[:LEN], out[LEN:])


def intra_back_kernel(meta, starts, fq, fk, v, scores, gnum, gden, mine, theirs, gfq, gfk, gval):
    low = low_lanes(LEN)
    even = jnp.where(low, 1.0, 0.0).astype(bf16)
    odd = jnp.where(low, 0.0, 1.0).astype(bf16)
    for row in range(fq.shape[0] // LEN):
        at = slice(row * LEN, (row + 1) * LEN)
        intra, cross, _ = masks_of(row, meta, starts)
        twice = jnp.concatenate([intra, intra], axis=0)
        blocks, norm = unpack_state(meta, mine, theirs, row)
        for pair in range(PAIRS):
            lanes = slice(pair * 128, (pair + 1) * 128)
            gn, gd, q, k = gnum[at, lanes], gden[at, lanes], fq[at, lanes], fk[at, lanes]
            both = jnp.concatenate([gn * even, gn * odd], axis=0)
            turned = pltpu.roll(gd, HEAD, 1)
            dens = jnp.concatenate(
                [jnp.where(low, gd, turned), jnp.where(low, turned, gd)], axis=0
            )
            gs = ((dot(both, v[at, lanes], NT) + dens) * twice).astype(bf16)
            near = dot(gs, k)
            far = cross_dot(gn, blocks[pair], NT) + gd * norm[:, lanes]
            gfq[at, lanes] = jnp.where(low, near[:LEN], near[LEN:]) + cross * far
            gfk[at, lanes] = jnp.where(low, dot(gs[:LEN], q, TN), dot(gs[LEN:], q, TN))
            sl = scores[row, pair]
            gval[at, lanes] = jnp.where(low, dot(sl[:LEN], gn, TN), dot(sl[LEN:], gn, TN))


def packed_back(meta, starts, mine, theirs, gfq, gfk, gval, fk, v, eq, ek, tables, dct, gp, gqb):
    tabs = tuple(t[...] for t in tables)
    high, low = dct[0][...], dct[1][...]
    for row in range(fk.shape[0] // LEN):
        at = slice(row * LEN, (row + 1) * LEN)
        tail = masks_of(row, meta, starts)[2]
        blocks, norm = unpack_state(meta, mine, theirs, row)
        keys, values = [], []
        for pair in range(PAIRS):
            lanes = slice(pair * 128, (pair + 1) * 128)
            far = cross_dot(v[at, lanes], blocks[pair], NT) + norm[:, lanes]
            keys.append(gfk[at, lanes] + tail * far)
            values.append(gval[at, lanes] + tail * cross_dot(fk[at, lanes], blocks[pair]))
        turned = tuple(t[at] for t in tabs)
        gp[at, :D] = unfeaturize(gfq[at] * eq[at], turned, high, low).astype(bf16)
        gk = jnp.concatenate(keys, axis=1)
        gp[at, D : 2 * D] = unfeaturize(gk * ek[at], turned, high, low).astype(bf16)
        gp[at, 2 * D :] = jnp.concatenate(values, axis=1).astype(bf16)
    gqb[...] = jnp.sum(gp[...].astype(f32), axis=0, keepdims=True)


def upstream_back(hidden, up, gfirst, gsecond, gain, ggain, gshift):
    xhat, inverse = norm_parts(hidden)
    gains = gain[...].astype(f32)
    one, ggain[0:1, :], gshift[0:1, :] = norm_back(gfirst, xhat, inverse, gains[0:1])
    two, ggain[1:2, :], gshift[1:2, :] = norm_back(gsecond, xhat, inverse, gains[1:2])
    return up + one + two


def turn_back_kernel(
    meta, starts, mine, theirs, gfq, gfk, gval, fk, v, eq, ek, ta, tb, tc, dh, dl, w, h, gain, gsecond, cot,
    ow, den, att, fq,
    gp, gqb, ggain, gshift, up_ref, up_low, gnum, gden, keep, send, gob,
):
    packed_back(
        meta, starts, mine, theirs, gfq, gfk, gval, fk, v, eq, ek, (ta, tb, tc), (dh, dl), gp, gqb
    )
    gfirst = dot(gp[...], w[...], NT)
    up = upstream_back(h[...], cot[...].astype(f32), gfirst, gsecond[...], gain, ggain, gshift)
    up_ref[...] = up
    low = up.astype(bf16)
    up_low[...] = low
    attend_back(meta, starts, low, ow, den, att, fq, gnum, gden, keep, send)
    gob[...] = jnp.sum(low.astype(f32), axis=0, keepdims=True)


def last_kernel(
    meta, starts, mine, theirs, gfq, gfk, gval, fk, v, eq, ek, ta, tb, tc, dh, dl, w, h, gain, gsecond, up,
    gp, gqb, ggain, gshift, ginputs,
):
    packed_back(
        meta, starts, mine, theirs, gfq, gfk, gval, fk, v, eq, ek, (ta, tb, tc), (dh, dl), gp, gqb
    )
    gfirst = dot(gp[...], w[...], NT)
    ginputs[...] = upstream_back(
        h[...].astype(f32), up[...], gfirst, gsecond[...], gain, ggain, gshift
    )


def reversed_bits(value, count):
    return sum(((value >> k) & 1) << (count - 1 - k) for k in range(count))


def gathered(size, meta, x, flat, held):
    count = size.bit_length() - 1
    block = flat.shape[0] // size
    flat[...] = x.astype(f32).T
    for place in range(size):
        source = reversed_bits(place, count) ^ meta[2]
        held[place * block : (place + 1) * block, :] = flat[
            pl.ds(pl.multiple_of(source * block, block), block), :
        ]
    return held[...].astype(bf16)


def feed_grad_kernel(size, meta, second, act, lift, up, in_keep, in_send, down_keep, down_send, f1, h1, f2, h2):
    left = gathered(size, meta, second[...], f1, h1)
    for k in range(2):
        for g in range(2):
            at = pl.multiple_of((k ^ meta[3]) * (FF // 2) + g * WIDE, WIDE)
            out = dot(left, lift[:, pl.ds(at, WIDE)])
            in_keep[k, :, g * WIDE : (g + 1) * WIDE] = out[: D // 2]
            in_send[k, :, g * WIDE : (g + 1) * WIDE] = out[D // 2 :]
    left = gathered(size, meta, act[...], f2, h2)
    for k in range(2):
        right = up[:, pl.ds(pl.multiple_of((k ^ meta[4]) * (D // 2), D // 2), D // 2)]
        for g in range(4):
            out = dot(left[g * WIDE : (g + 1) * WIDE], right)
            ref = (down_keep, down_send)[g // 2]
            ref[k, (g % 2) * WIDE : (g % 2 + 1) * WIDE, :] = out


def packed_grad_kernel(size, meta, first, att_low, gp, up, a_keep, a_send, b_keep, b_send, f1, h1):
    for source, wide, begin in ((first, 384, 0), (att_low, 128, 384)):
        left = gathered(size, meta, source[...], f1, h1)
        right = gp if wide == 384 else up
        for part, (keep, send) in enumerate(((a_keep, a_send), (b_keep, b_send))):
            for k in range(2):
                at = pl.multiple_of((2 * part + (k ^ meta[3 + part])) * wide, wide)
                out = dot(left, right[:, pl.ds(at, wide)])
                keep[k, :, begin : begin + wide] = out[: D // 2]
                send[k, :, begin : begin + wide] = out[D // 2 :]


class Layer:
    def __init__(self, array, index):
        self.array, self.index = array, index


class Scalars:
    def __init__(self, array):
        self.array = array


def call(kernel, name, operands, outs, flops, scratch=()):
    specs, arrays = [], []
    for operand in operands:
        if isinstance(operand, Scalars):
            specs.append(pl.BlockSpec(memory_space=pltpu.SMEM))
            arrays.append(operand.array)
        elif isinstance(operand, Layer):
            array, index = operand.array, operand.index
            rest = array.shape[1:]
            specs.append(
                pl.BlockSpec(
                    (None,) + rest, lambda i, n=len(rest), index=index: (index,) + (0,) * n
                )
            )
            arrays.append(array)
        else:
            specs.append(pl.BlockSpec(operand.shape, lambda i, n=operand.ndim: (0,) * n))
            arrays.append(operand)
    moved = sum(a.size * a.dtype.itemsize for a in arrays)
    moved += sum(math.prod(o.shape) * o.dtype.itemsize for o in outs)
    return pl.pallas_call(
        kernel,
        name=name,
        grid=(1,),
        in_specs=specs,
        out_specs=[pl.BlockSpec(o.shape, lambda i, n=len(o.shape): (0,) * n) for o in outs],
        out_shape=list(outs),
        scratch_shapes=list(scratch),
        cost_estimate=pl.CostEstimate(flops=int(flops), bytes_accessed=moved, transcendentals=0),
        compiler_params=pltpu.CompilerParams(vmem_limit_bytes=40 * 1024 * 1024),
    )(*arrays)


def cosine_table():
    frequency = np.arange(HEAD, dtype=np.float64)[:, None]
    columns = np.arange(HEAD, dtype=np.float64)[None, :]
    entries = np.cos(math.pi * (2.0 * columns + 1.0) * frequency / (2.0 * HEAD))
    entries = entries * math.sqrt(2.0 / HEAD)
    entries[0] *= math.sqrt(0.5)
    wide = np.kron(np.eye(4), entries.T)
    high = wide.astype(np.float32).astype(bf16)
    low = (wide.astype(np.float32) - high.astype(np.float32)).astype(bf16)
    return jnp.asarray(high), jnp.asarray(low)


def rotary_tables(places):
    lane = jnp.arange(128) % HEAD
    half = ROT // 2
    inverse = 10000.0 ** (-((lane % half).astype(f32) * 2.0 / ROT))
    inverse = jnp.where(lane < ROT, inverse, 0.0)
    angles = places.astype(f32)[:, None] * inverse[None, :]
    sine = jnp.sin(angles)
    ahead = jnp.where(lane < half, -sine, 0.0)
    behind = jnp.where((lane >= half) & (lane < ROT), sine, 0.0)
    return jnp.cos(angles), ahead, behind


def flip(value, axis, bit):
    size = lax.axis_size(axis)
    return lax.ppermute(value, axis, [(i, i ^ bit) for i in range(size)])


def chips_on(value, step):
    size = lax.axis_size("seq")
    pairs = [(i, i + 2 * step) for i in range(size) if 0 <= i + 2 * step < size]
    return lax.ppermute(value, "seq", pairs)


def exchange(keep, send, flag, core, chip, backward):
    chips = lax.axis_size("seq") // 2
    begin, span = chip * 2 * LEN, 2 * LEN
    got = flip(send, "seq", 1)
    even, odd = jnp.where(core == 0, keep, got), jnp.where(core == 0, got, keep)
    sign = -1 if backward else 1
    if backward:
        whole = even + flag(begin + LEN - 1, begin) * odd
    else:
        whole = odd + flag(begin + span - 1, begin + LEN) * even
    entered = chips_on(whole, sign)
    step = 2
    while step < chips:
        partial = whole + flag(begin + span - 1, begin) * entered
        more = chips_on(partial, sign * step)
        if backward:
            entered = entered + flag(begin + span * step - 1, begin + span) * more
        else:
            entered = entered + flag(begin - 1, begin - span * (step - 1)) * more
        step *= 2
    if backward:
        for_even, for_odd = odd + flag(begin + span - 1, begin + LEN) * entered, entered
    else:
        for_even, for_odd = entered, even + flag(begin + LEN - 1, begin) * entered
    mine = jnp.where(core == 0, for_even, for_odd)
    theirs = flip(jnp.where(core == 0, for_odd, for_even), "seq", 1)
    return mine, theirs


def reduce_chunk(keep, send, bit):
    size = lax.axis_size("seq")
    got = flip(send, "seq", 1)
    got_first = flip(keep[1] + got[1], "batch", bit)
    total = keep[0] + got[0] + got_first
    step = 2
    while step < size:
        half = total.shape[0] // 2
        total = total[:half] + flip(total[half:], "seq", step)
        step *= 2
    total = total + flip(total, "batch", 3 - bit)
    return total, flip(total, "batch", bit)


def per_device(
    inputs,
    doc_starts,
    cotangent,
    norm_gain,
    norm_bias,
    qkv_weight,
    qkv_bias,
    out_weight,
    out_bias,
    in_weight,
    in_bias,
    down_weight,
    down_bias,
):
    rows, length = inputs.shape[0], inputs.shape[1]
    tokens = rows * length
    size = lax.axis_size("seq")
    me, column = lax.axis_index("seq"), lax.axis_index("batch")
    core, chip = me % 2, me // 2
    bits = (column % 2, column // 2)
    begin = me * length
    absolute = begin + jnp.arange(length, dtype=jnp.int32)

    def segment_at(position):
        return jnp.max(jnp.where(doc_starts <= position, doc_starts, 0), axis=1)

    def flag(position, limit):
        return (segment_at(position) < limit).astype(f32)[:, None, None]

    segment = jnp.max(
        jnp.where(doc_starts[:, None, :] <= absolute[None, :, None], doc_starts[:, None, :], 0),
        axis=2,
    )
    tables = rotary_tables((absolute[None, :] - segment).reshape(tokens))
    dct = cosine_table()
    meta = Scalars(jnp.stack([begin, core, me, bits[0], bits[1]]).astype(jnp.int32))
    starts = Scalars(doc_starts)
    hidden0 = inputs.reshape(tokens, D)
    cot = cotangent.reshape(tokens, D)
    out_bias2, in_bias2, down_bias2 = (
        out_bias[:, None, :],
        in_bias[:, None, :],
        down_bias[:, None, :],
    )

    tall, fat = sds((tokens, D)), sds((tokens, D), bf16)
    packed_state = sds((rows, PACK, 128))
    front_outs = [fat, fat, fat, fat, fat, tall, tall, packed_state, packed_state]
    matmul = 2.0 * tokens * D * D

    def front_of(layer):
        return [
            Layer(norm_gain, layer),
            Layer(norm_bias, layer),
            Layer(qkv_weight, layer),
            Layer(qkv_bias, layer),
            *tables,
            *dct,
        ]

    first, second, fq, fk, v, eq, ek, keep, send = call(
        front_kernel, "front", [meta, starts, hidden0, *front_of(0)], front_outs, 6 * matmul
    )
    entered0 = exchange(keep, send, flag, core, chip, False)
    feed_weights = [
        [Layer(x, layer) for x in (in_weight, in_bias2, down_weight, down_bias2)]
        for layer in range(2)
    ]
    act0, slope0, feed0 = call(
        feed_kernel,
        "feed",
        [second, *feed_weights[0]],
        [sds((tokens, FF), bf16), sds((tokens, FF)), tall],
        8 * matmul,
    )
    intra_outs = [sds((rows, PAIRS, 2 * LEN, LEN), bf16), tall, tall]
    scores0, num0, kt0 = call(
        intra_kernel, "intra", [meta, starts, fq, fk, v], intra_outs, 2 * matmul
    )
    first0, second0, fq0, fk0, v0, eq0, ek0 = first, second, fq, fk, v, eq, ek
    den0, att0, att_low0, hidden1, first1, second1, fq1, fk1, v1, eq1, ek1, keep, send = call(
        middle_kernel,
        "middle",
        [meta, starts, hidden0, feed0, num0, kt0, fq0, *entered0]
        + [Layer(out_weight, 0), Layer(out_bias2, 0), *front_of(1)],
        [tall, tall, fat, tall] + front_outs,
        8 * matmul,
    )
    entered1 = exchange(keep, send, flag, core, chip, False)
    act1, feed1, lift1, gsecond1, gib1 = call(
        feed_both_kernel,
        "feed_both",
        [second1, *feed_weights[1], cot],
        [sds((tokens, FF), bf16), tall, sds((tokens, FF), bf16), tall, sds((1, FF))],
        16 * matmul,
    )
    scores1, num1, kt1 = call(
        intra_kernel, "intra", [meta, starts, fq1, fk1, v1], intra_outs, 2 * matmul
    )

    def feed_grad(second, act, lift, up):
        wide, narrow = sds((2, D // 2, FF // 2)), sds((2, FF // 2, D // 2))
        flat = [pltpu.VMEM((D, tokens), f32)] * 2 + [pltpu.VMEM((FF, tokens), f32)] * 2
        a_keep, a_send, b_keep, b_send = call(
            functools.partial(feed_grad_kernel, size),
            "feed_grad",
            [meta, second, act, lift, up],
            [wide, wide, narrow, narrow],
            8 * matmul,
            flat,
        )
        return reduce_chunk(a_keep, a_send, 1), reduce_chunk(b_keep, b_send, 2)

    chunk_feed1 = feed_grad(second1, act1, lift1, cot)
    den1, att1, att_low1, result, gnum1, gden1, keep, send, gob1 = call(
        turn_kernel,
        "turn",
        [meta, starts, hidden1, feed1, num1, kt1, fq1, *entered1]
        + [Layer(out_weight, 1), Layer(out_bias2, 1), cot],
        [tall, tall, fat, fat, fat, tall, packed_state, packed_state, sds((1, D))],
        3 * matmul,
    )
    later1 = exchange(keep, send, flag, core, chip, True)
    gfq1, gfk1, gval1 = call(
        intra_back_kernel,
        "intra_back",
        [meta, starts, fq1, fk1, v1, scores1, gnum1, gden1, *entered1],
        [tall, tall, tall],
        4 * matmul,
    )
    vector_outs = [sds((1, 3 * D)), sds((2, D)), sds((2, D))]
    packed = sds((tokens, 3 * D), bf16)
    gp1, gqb1, ggain1, gshift1, up0, up_low0, gnum0, gden0, keep, send, gob0 = call(
        turn_back_kernel,
        "turn_back",
        [meta, starts, *later1, gfq1, gfk1, gval1, fk1, v1, eq1, ek1, *tables, *dct]
        + [Layer(qkv_weight, 1), hidden1, Layer(norm_gain, 1), gsecond1, cot]
        + [Layer(out_weight, 0), den0, att0, fq0],
        [packed, *vector_outs, tall, fat, fat, tall, packed_state, packed_state, sds((1, D))],
        8 * matmul,
    )
    later0 = exchange(keep, send, flag, core, chip, True)
    lift0, gsecond0, gib0 = call(
        feed_back_kernel,
        "feed_back",
        [slope0, up_low0, Layer(in_weight, 0), Layer(down_weight, 0)],
        [sds((tokens, FF), bf16), tall, sds((1, FF))],
        8 * matmul,
    )
    gfq0, gfk0, gval0 = call(
        intra_back_kernel,
        "intra_back",
        [meta, starts, fq0, fk0, v0, scores0, gnum0, gden0, *entered0],
        [tall, tall, tall],
        4 * matmul,
    )

    def packed_grad(first, att_low, gp, up):
        quarter = sds((2, D // 2, D))
        flat = [pltpu.VMEM((D, tokens), f32)] * 2
        return call(
            functools.partial(packed_grad_kernel, size),
            "packed_grad",
            [meta, first, att_low, gp, up],
            [quarter] * 4,
            4 * matmul,
            flat,
        )

    a_keep, a_send, b_keep, b_send = packed_grad(first1, att_low1, gp1, cot)
    chunk_packed1 = reduce_chunk(a_keep, a_send, 1), reduce_chunk(b_keep, b_send, 2)
    chunk_feed0 = feed_grad(second0, act0, lift0, up_low0)
    gp0, gqb0, ggain0, gshift0, ginputs = call(
        last_kernel,
        "last",
        [meta, starts, *later0, gfq0, gfk0, gval0, fk0, v0, eq0, ek0, *tables, *dct]
        + [Layer(qkv_weight, 0), hidden0, Layer(norm_gain, 0), gsecond0, up0],
        [packed, *vector_outs, tall],
        6 * matmul,
    )
    a_keep, a_send, b_keep, b_send = packed_grad(first0, att_low0, gp0, up_low0)

    slot = D // size
    vectors = jnp.concatenate(
        [
            part.reshape(-1, size, slot)
            if part.shape[-1] != FF
            else part.reshape(size, FF // D, slot).swapaxes(0, 1)
            for layer in (
                (ggain0, gshift0, gqb0.reshape(3, D), gob0, gib0),
                (ggain1, gshift1, gqb1.reshape(3, D), gob1, gib1),
            )
            for part in layer
        ],
        axis=0,
    ).swapaxes(0, 1)
    count = size.bit_length() - 1
    order = np.array([reversed_bits(k, count) for k in range(size)], np.int32) ^ me
    vectors = jnp.take(vectors, order, axis=0).reshape(size, 2, -1)
    vectors = jnp.where(bits[0] == 0, vectors, vectors[:, ::-1]).swapaxes(0, 1)
    held = vectors.shape[2]
    under = -(-held // (8 * D)) * 8
    vectors = jnp.pad(vectors, ((0, 0), (0, 0), (0, under * D - held)))
    vectors = vectors.reshape(2, size, under, D)

    def with_vectors(part, lines):
        part = part.reshape(2, size // 2, slot, D)
        return jnp.concatenate([part, lines], axis=2).reshape(2, -1, D)

    a_keep = with_vectors(a_keep, vectors[:, : size // 2])
    a_send = with_vectors(a_send, vectors[:, size // 2 :])
    own, other = reduce_chunk(a_keep, a_send, 1)
    chunk_packed0 = (own[:slot], other[:slot]), reduce_chunk(b_keep, b_send, 2)
    lines = [part[slot:].reshape(-1)[:held] for part in (own, other)]
    summed = jnp.where(
        bits[0] == 0, jnp.concatenate(lines), jnp.concatenate(lines[::-1])
    ).reshape(2, 12, slot)

    def joined(chunk, bit):
        own, other = chunk
        return jnp.where(
            bit == 0,
            jnp.concatenate([own, other], axis=-1),
            jnp.concatenate([other, own], axis=-1),
        )

    def of_layers(make):
        return jnp.stack([make(0), make(1)])

    chunks_feed, chunks_packed = (chunk_feed0, chunk_feed1), (chunk_packed0, chunk_packed1)

    def columns(layer, begin, wide):
        pieces = []
        for part in range(2):
            own, other = chunks_packed[layer][part]
            pieces.append(
                joined((own[:, begin : begin + wide], other[:, begin : begin + wide]), bits[part])
            )
        return jnp.concatenate(pieces, axis=-1)

    grad_gain, grad_shift = summed[:, 0:2], summed[:, 2:4]
    grad_qkv_b, grad_out_b = summed[:, 4:7], summed[:, 7]
    grad_in_b = summed[:, 8:12].reshape(2, FF // size)
    return (
        result.reshape(rows, length, D),
        ginputs.reshape(rows, length, D),
        grad_gain,
        grad_shift,
        of_layers(lambda layer: columns(layer, 0, 384)),
        grad_qkv_b,
        of_layers(lambda layer: columns(layer, 384, 128)),
        grad_out_b,
        of_layers(lambda layer: joined(chunks_feed[layer][0], bits[0])),
        grad_in_b,
        of_layers(lambda layer: joined(chunks_feed[layer][1], bits[1])),
        grad_out_b,
    )


def solution(mesh):
    placed = (
        P("batch", "seq", None),
        P("batch", None),
        P("batch", "seq", None),
        P(),
        P(),
        P(),
        P(),
        P(),
        P(),
        P(),
        P(),
        P(),
        P(),
    )
    return jax.shard_map(
        per_device,
        mesh=mesh,
        in_specs=placed,
        out_specs=(
            P("batch", "seq", None),
            P("batch", "seq", None),
            P(None, None, "seq"),
            P(None, None, "seq"),
            P(None, "seq", None),
            P(None, None, "seq"),
            P(None, "seq", None),
            P(None, "seq"),
            P(None, "seq", None),
            P(None, "seq"),
            P(None, "seq", None),
            P(None, "seq"),
        ),
        check_vma=False,
    )
```

time: 880 us -> 448 us (0.51)
  waiting for transfers between devices: 458 us -> 166 us
  matrix products: 96.5 us -> 0 us
  blocking collectives: 92.5 us -> 0 us
  starting transfers between devices: 1.55 us -> 82.5 us
  other arithmetic: 113 us -> 52.6 us
  Pallas kernels: 0 us -> 41.4 us
  between operations: 17.5 us -> 3.1 us
    reduce_scatter x4 -> x0, waiting for transfers between devices: 225 us -> none  [the longest x1 90.3 us: per_device(): lax.psum_scatter(sum_down, 'seq', scatter_dimension=1, tiled=True)]
    ppermute x0 -> x64, waiting for transfers between devices: none -> 166 us  [the longest x56 138 us: flip(): return lax.ppermute(value, axis, [(i, i ^ bit) for i in range(size)])]
    unnamed x19 -> x0, waiting for transfers between devices: 149 us -> none
    dot_general x62 -> x0, matrix products: 96.5 us -> none  [the longest x8 12.3 us: featurize(): jnp.einsum('bthj,fj->bthf', rotate(heads_x, places), cosines, precision=P...]
    ppermute x0 -> x64, starting transfers between devices: none -> 82.5 us  [the longest x56 55.2 us: flip(): return lax.ppermute(value, axis, [(i, i ^ bit) for i in range(size)])]
    psum x1 -> x0, waiting for transfers between devices: 70.9 us -> none  [per_device(): lax.psum((row_parts[0], row_parts[1], row_parts[2], row_parts[3], row_par...]
    all_gather x4 -> x0, blocking collectives: 57 us -> none  [entering(): everything = jax.tree.map(lambda part: lax.all_gather(part, axis), value)]
    unnamed x337 -> x338, local copies, waits for them, and re-layouts: 32.2 us -> 74.5 us
  transfers between devices with their start and end apart: 14 -> 64, of which waited for: 10 -> 33; matrix products, arithmetic and copies ran while one was open for 19% -> 15% of each run, Pallas kernels for 0% -> 7%
where the time goes in v1:
time: 448 us; the launch traced here: 439 us
  waiting for transfers between devices  166 us (37%)
  local copies, waits for them, and re-layouts  93.7 us (21%)
  starting transfers between devices  82.5 us (18%)
  other arithmetic  52.6 us (12%)
  Pallas kernels  41.4 us (9%)
    ppermute x56, waiting for transfers between devices, flip(): return lax.ppermute(value, axis, [(i, i ^ bit) for i in range(size)])  138 us
    unnamed x338, local copies, waits for them, and re-layouts  74.5 us
    ppermute x56, starting transfers between devices, flip(): return lax.ppermute(value, axis, [(i, i ^ bit) for i in range(size)])  55.2 us
    pallas_call x16, Pallas kernels, call(): pl.pallas_call(kernel, name=name, grid=(1,), in_specs=specs, out_specs=[p...  41.4 us
    ppermute x8, waiting for transfers between devices, chips_on(): return lax.ppermute(value, 'seq', pairs)  28.3 us
    ppermute x8, starting transfers between devices, chips_on(): return lax.ppermute(value, 'seq', pairs)  27.3 us
    pallas_call x6, other arithmetic, call(): pl.pallas_call(kernel, name=name, grid=(1,), in_specs=specs, out_specs=[p...  9.78 us
    add x8, other arithmetic, reduce_chunk(): total = keep[0] + got[0] + got_first  9.76 us
  transfers between devices with their start and end apart: 64, of which 33 were waited for; matrix products, arithmetic and copies ran while one was open for 15% of the time, Pallas kernels for 7%

profile of v1, /device:TPU:0, one launch (start us, length us, event | category | flops | bytes accessed | tf_op | source)
XLA Modules:
  0.0 439.3 jit_solution(5268030194110810869)
XLA Ops:
  15.4 4.8 %collective-permute-start.1 = (f32[2,136,128]{2,1,0:T(8,128)S(1)}, f32[2,136,128]{2,1,0:T(8,128)S(1)}, u32[]{:S(2)}, u32[]{:S(2)}) collective-permute-start(f32[2,136,128]{2,1,0:T(8,128)S(1)} %multiply_add_fusion.15), channel_id=1, source_target_pairs={{0,2},{1,3},{2,4},{3,5},{4,6},{5,7},{8,10},{9,11},{10,12},{11,13},... | collective-permute-start | bytes 417800 | tf_op jit(solution)/shard_map/ppermute | solution.py:560
  20.2 3.2 collective-permute-done.1
  23.5 5.4 %collective-permute-start.2 = (f32[2,136,128]{2,1,0:T(8,128)S(1)}, f32[2,136,128]{2,1,0:T(8,128)S(1)}, u32[]{:S(2)}, u32[]{:S(2)}) collective-permute-start(f32[2,136,128]{2,1,0:T(8,128)S(1)} %multiply_add_fusion.14), channel_id=1, source_target_pairs={{0,4},{1,5},{2,6},{3,7},{8,12},{9,13},{10,14},{11,15},{16,20},{17,... | collective-permute-start | bytes 417800 | tf_op jit(solution)/shard_map/ppermute | solution.py:560
  46.4 3.5 middle.1
  55.3 6.2 %collective-permute-start.5 = (f32[2,136,128]{2,1,0:T(8,128)S(1)}, f32[2,136,128]{2,1,0:T(8,128)S(1)}, u32[]{:S(2)}, u32[]{:S(2)}) collective-permute-start(f32[2,136,128]{2,1,0:T(8,128)S(1)} %multiply_add_fusion.11), channel_id=1, source_target_pairs={{0,2},{1,3},{2,4},{3,5},{4,6},{5,7},{8,10},{9,11},{10,12},{11,13},... | collective-permute-start | bytes 417800 | tf_op jit(solution)/shard_map/ppermute | solution.py:560
  61.5 3.4 collective-permute-done.5
  65.0 5.5 %collective-permute-start.6 = (f32[2,136,128]{2,1,0:T(8,128)S(1)}, f32[2,136,128]{2,1,0:T(8,128)S(1)}, u32[]{:S(2)}, u32[]{:S(2)}) collective-permute-start(f32[2,136,128]{2,1,0:T(8,128)S(1)} %multiply_add_fusion.10), channel_id=1, source_target_pairs={{0,4},{1,5},{2,6},{3,7},{8,12},{9,13},{10,14},{11,15},{16,20},{17,... | collective-permute-start | bytes 417800 | tf_op jit(solution)/shard_map/ppermute | solution.py:560
  85.8 9.5 %collective-permute-done.9 = f32[2,136,128]{2,1,0:T(8,128)} collective-permute-done((f32[2,136,128]{2,1,0:T(8,128)}, f32[2,136,128]{2,1,0:T(8,128)}, u32[]{:S(2)}, u32[]{:S(2)}) %collective-permute-start.9) | collective-permute-done | bytes 139296 | tf_op jit(solution)/shard_map/ppermute | solution.py:560
  98.3 9.2 %collective-permute-done.10 = f32[2,136,128]{2,1,0:T(8,128)S(1)} collective-permute-done((f32[2,136,128]{2,1,0:T(8,128)S(1)}, f32[2,136,128]{2,1,0:T(8,128)S(1)}, u32[]{:S(2)}, u32[]{:S(2)}) %collective-permute-start.10) | collective-permute-done | bytes 139296 | tf_op jit(solution)/shard_map/ppermute | solution.py:560
  123.3 3.7 turn_back.1
  199.5 3.9 last.1
  227.0 8.5 %collective-permute-done.35 = f32[256,512]{1,0:T(8,128)S(1)} collective-permute-done((f32[256,512]{1,0:T(8,128)S(1)}, f32[256,512]{1,0:T(8,128)S(1)}, u32[]{:S(2)}, u32[]{:S(2)}) %collective-permute-start.35) | collective-permute-done | bytes 524320 | tf_op jit(solution)/shard_map/ppermute | solution.py:554
  243.6 6.9 %collective-permute-done.36 = f32[128,512]{1,0:T(8,128)S(1)} collective-permute-done((f32[128,512]{1,0:T(8,128)S(1)}, f32[128,512]{1,0:T(8,128)S(1)}, u32[]{:S(2)}, u32[]{:S(2)}) %collective-permute-start.36) | collective-permute-done | bytes 262176 | tf_op jit(solution)/shard_map/ppermute | solution.py:554
  251.0 3.4 collective-permute-done.30
  254.3 4.2 collective-permute-start.37
  258.6 4.8 %collective-permute-done.37 = f32[64,512]{1,0:T(8,128)S(1)} collective-permute-done((f32[64,512]{1,0:T(8,128)S(1)}, f32[64,512]{1,0:T(8,128)S(1)}, u32[]{:S(2)}, u32[]{:S(2)}) %collective-permute-start.37) | collective-permute-done | bytes 131104 | tf_op jit(solution)/shard_map/ppermute | solution.py:554
  264.6 4.9 %collective-permute-done.31 = f32[64,512]{1,0:T(8,128)S(1)} collective-permute-done((f32[64,512]{1,0:T(8,128)S(1)}, f32[64,512]{1,0:T(8,128)S(1)}, u32[]{:S(2)}, u32[]{:S(2)}) %collective-permute-start.31) | collective-permute-done | bytes 131104 | tf_op jit(solution)/shard_map/ppermute | solution.py:554
  269.4 5.0 %collective-permute-start.23 = (f32[256,512]{1,0:T(8,128)S(1)}, f32[256,512]{1,0:T(8,128)S(1)}, u32[]{:S(2)}, u32[]{:S(2)}) collective-permute-start(f32[256,512]{1,0:T(8,128)S(1)} %fusion.22), channel_id=1, source_target_pairs={{0,16},{8,24},{16,0},{24,8},{1,17},{9,25},{17,1},{25,9},{2,18},{10... | collective-permute-start | bytes 1572872 | tf_op jit(solution)/shard_map/ppermute | solution.py:554
  281.5 5.5 %collective-permute-done.32 = f32[64,512]{1,0:T(8,128)S(1)} collective-permute-done((f32[64,512]{1,0:T(8,128)S(1)}, f32[64,512]{1,0:T(8,128)S(1)}, u32[]{:S(2)}, u32[]{:S(2)}) %collective-permute-start.32) | collective-permute-done | bytes 131104 | tf_op jit(solution)/shard_map/ppermute | solution.py:554
  295.1 4.4 %collective-permute-done.33 = f32[64,512]{1,0:T(8,128)S(1)} collective-permute-done((f32[64,512]{1,0:T(8,128)S(1)}, f32[64,512]{1,0:T(8,128)S(1)}, u32[]{:S(2)}, u32[]{:S(2)}) %collective-permute-start.33) | collective-permute-done | bytes 131104 | tf_op jit(solution)/shard_map/ppermute | solution.py:554
  303.0 13.4 %collective-permute-done.24 = f32[128,512]{1,0:T(8,128)S(1)} collective-permute-done((f32[128,512]{1,0:T(8,128)S(1)}, f32[128,512]{1,0:T(8,128)S(1)}, u32[]{:S(2)}, u32[]{:S(2)}) %collective-permute-start.24) | collective-permute-done | bytes 262176 | tf_op jit(solution)/shard_map/ppermute | solution.py:554
  318.2 3.4 collective-permute-start.25
  321.8 4.2 collective-permute-done.25
  327.3 8.2 %collective-permute-done.18 = f32[144,512]{1,0:T(8,128)S(1)} collective-permute-done((f32[144,512]{1,0:T(8,128)S(1)}, f32[144,512]{1,0:T(8,128)S(1)}, u32[]{:S(2)}, u32[]{:S(2)}) %collective-permute-start.18) | collective-permute-done | bytes 294944 | tf_op jit(solution)/shard_map/ppermute | solution.py:554
  340.9 16.6 %collective-permute-done.19 = f32[72,512]{1,0:T(8,128)S(1)} collective-permute-done((f32[72,512]{1,0:T(8,128)S(1)}, f32[72,512]{1,0:T(8,128)S(1)}, u32[]{:S(2)}, u32[]{:S(2)}) %collective-permute-start.19) | collective-permute-done | bytes 147488 | tf_op jit(solution)/shard_map/ppermute | solution.py:554
  357.5 6.2 %collective-permute-done.27 = f32[64,512]{1,0:T(8,128)S(1)} collective-permute-done((f32[64,512]{1,0:T(8,128)S(1)}, f32[64,512]{1,0:T(8,128)S(1)}, u32[]{:S(2)}, u32[]{:S(2)}) %collective-permute-start.27) | collective-permute-done | bytes 131104 | tf_op jit(solution)/shard_map/ppermute | solution.py:554
  370.1 5.9 %collective-permute-done.21 = f32[72,512]{1,0:T(8,128)S(1)} collective-permute-done((f32[72,512]{1,0:T(8,128)S(1)}, f32[72,512]{1,0:T(8,128)S(1)}, u32[]{:S(2)}, u32[]{:S(2)}) %collective-permute-start.21) | collective-permute-done | bytes 147488 | tf_op jit(solution)/shard_map/ppermute | solution.py:554
  385.0 10.8 %collective-permute-done.42 = f32[128,1024]{1,0:T(8,128)S(1)} collective-permute-done((f32[128,1024]{1,0:T(8,128)S(1)}, f32[128,1024]{1,0:T(8,128)S(1)}, u32[]{:S(2)}, u32[]{:S(2)}) %collective-permute-start.42) | collective-permute-done | bytes 524320 | tf_op jit(solution)/shard_map/ppermute | solution.py:554
  396.7 5.8 %collective-permute-done.54 = f32[512,256]{1,0:T(8,128)S(1)} collective-permute-done((f32[512,256]{1,0:T(8,128)S(1)}, f32[512,256]{1,0:T(8,128)S(1)}, u32[]{:S(2)}, u32[]{:S(2)}) %collective-permute-start.54) | collective-permute-done | bytes 524320 | tf_op jit(solution)/shard_map/ppermute | solution.py:554
  402.5 3.7 collective-permute-start.55
  406.3 9.3 %collective-permute-done.43 = f32[64,1024]{1,0:T(8,128)S(1)} collective-permute-done((f32[64,1024]{1,0:T(8,128)S(1)}, f32[64,1024]{1,0:T(8,128)S(1)}, u32[]{:S(2)}, u32[]{:S(2)}) %collective-permute-start.43) | collective-permute-done | bytes 262176 | tf_op jit(solution)/shard_map/ppermute | solution.py:554
  423.6 4.3 collective-permute-done.51
  (612 shorter events, 238.3 us)
Async XLA Ops:
  140.2 76.8 %collective-permute-start.46 = (f32[2,256,1024]{2,1,0:T(8,128)}, f32[2,256,1024]{2,1,0:T(8,128)}, u32[]{:S(2)}, u32[]{:S(2)}) collective-permute-start(f32[2,256,1024]{2,1,0:T(8,128)} %get-tuple-element.175), channel_id=1, source_target_pairs={{0,1},{1,0},{2,3},{3,2},{4,5},{5,4},{6,7},{7,6},{8,9},{9,8},{10,11... | collective-permute-start | bytes 6291464 | tf_op jit(solution)/shard_map/ppermute | solution.py:554
  141.0 13.9 %collective-permute-start.13 = (f32[2,136,128]{2,1,0:T(8,128)}, f32[2,136,128]{2,1,0:T(8,128)}, u32[]{:S(2)}, u32[]{:S(2)}) collective-permute-start(f32[2,136,128]{2,1,0:T(8,128)} %multiply_add_fusion.3), channel_id=1, source_target_pairs={{2,0},{3,1},{4,2},{5,3},{6,4},{7,5},{10,8},{11,9},{12,10},{13,11},... | collective-permute-start | bytes 417800 | tf_op jit(solution)/shard_map/ppermute | solution.py:560
  147.9 76.1 %collective-permute-start.58 = (f32[2,1024,256]{2,1,0:T(8,128)}, f32[2,1024,256]{2,1,0:T(8,128)}, u32[]{:S(2)}, u32[]{:S(2)}) collective-permute-start(f32[2,1024,256]{2,1,0:T(8,128)} %copy-done.124), channel_id=1, source_target_pairs={{0,1},{1,0},{2,3},{3,2},{4,5},{5,4},{6,7},{7,6},{8,9},{9,8},{10,11... | collective-permute-start | bytes 6291464 | tf_op jit(solution)/shard_map/ppermute | solution.py:554
  156.7 33.8 %collective-permute-start.14 = (f32[2,136,128]{2,1,0:T(8,128)}, f32[2,136,128]{2,1,0:T(8,128)}, u32[]{:S(2)}, u32[]{:S(2)}) collective-permute-start(f32[2,136,128]{2,1,0:T(8,128)} %multiply_add_fusion.2), channel_id=1, source_target_pairs={{4,0},{5,1},{6,2},{7,3},{12,8},{13,9},{14,10},{15,11},{20,16},{21,... | collective-permute-start | bytes 417800 | tf_op jit(solution)/shard_map/ppermute | solution.py:560
  189.8 30.0 %collective-permute-start.34 = (f32[2,256,512]{2,1,0:T(8,128)}, f32[2,256,512]{2,1,0:T(8,128)}, u32[]{:S(2)}, u32[]{:S(2)}) collective-permute-start(f32[2,256,512]{2,1,0:T(8,128)} %get-tuple-element.167), channel_id=1, source_target_pairs={{0,1},{1,0},{2,3},{3,2},{4,5},{5,4},{6,7},{7,6},{8,9},{9,8},{10,11... | collective-permute-start | bytes 3145736 | tf_op jit(solution)/shard_map/ppermute | solution.py:554
  189.9 31.2 %collective-permute-start.28 = (f32[2,256,512]{2,1,0:T(8,128)}, f32[2,256,512]{2,1,0:T(8,128)}, u32[]{:S(2)}, u32[]{:S(2)}) collective-permute-start(f32[2,256,512]{2,1,0:T(8,128)} %get-tuple-element.165), channel_id=1, source_target_pairs={{0,1},{1,0},{2,3},{3,2},{4,5},{5,4},{6,7},{7,6},{8,9},{9,8},{10,11... | collective-permute-start | bytes 3145736 | tf_op jit(solution)/shard_map/ppermute | solution.py:554
  199.0 89.5 %collective-permute-start.40 = (f32[2,256,1024]{2,1,0:T(8,128)}, f32[2,256,1024]{2,1,0:T(8,128)}, u32[]{:S(2)}, u32[]{:S(2)}) collective-permute-start(f32[2,256,1024]{2,1,0:T(8,128)} %get-tuple-element.171), channel_id=1, source_target_pairs={{0,1},{1,0},{2,3},{3,2},{4,5},{5,4},{6,7},{7,6},{8,9},{9,8},{10,11... | collective-permute-start | bytes 6291464 | tf_op jit(solution)/shard_map/ppermute | solution.py:554
  217.0 26.4 %collective-permute-start.16 = (f32[2,288,512]{2,1,0:T(8,128)S(1)}, f32[2,288,512]{2,1,0:T(8,128)S(1)}, u32[]{:S(2)}, u32[]{:S(2)}) collective-permute-start(f32[2,288,512]{2,1,0:T(8,128)S(1)} %bitcast.119), channel_id=1, source_target_pairs={{0,1},{1,0},{2,3},{3,2},{4,5},{5,4},{6,7},{7,6},{8,9},{9,8},{10,11... | collective-permute-start | bytes 3538952 | tf_op jit(solution)/shard_map/ppermute | solution.py:554
  219.8 21.0 %collective-permute-start.22 = (f32[2,256,512]{2,1,0:T(8,128)S(1)}, f32[2,256,512]{2,1,0:T(8,128)S(1)}, u32[]{:S(2)}, u32[]{:S(2)}) collective-permute-start(f32[2,256,512]{2,1,0:T(8,128)S(1)} %get-tuple-element.160), channel_id=1, source_target_pairs={{0,1},{1,0},{2,3},{3,2},{4,5},{5,4},{6,7},{7,6},{8,9},{9,8},{10,11... | collective-permute-start | bytes 3145736 | tf_op jit(solution)/shard_map/ppermute | solution.py:554
  221.2 14.3 %collective-permute-start.35 = (f32[256,512]{1,0:T(8,128)S(1)}, f32[256,512]{1,0:T(8,128)S(1)}, u32[]{:S(2)}, u32[]{:S(2)}) collective-permute-start(f32[256,512]{1,0:T(8,128)S(1)} %fusion.16), channel_id=1, source_target_pairs={{0,16},{8,24},{16,0},{24,8},{1,17},{9,25},{17,1},{25,9},{2,18},{10... | collective-permute-start | bytes 1572872 | tf_op jit(solution)/shard_map/ppermute | solution.py:554
  224.0 14.0 %collective-permute-start.29 = (f32[256,512]{1,0:T(8,128)S(1)}, f32[256,512]{1,0:T(8,128)S(1)}, u32[]{:S(2)}, u32[]{:S(2)}) collective-permute-start(f32[256,512]{1,0:T(8,128)S(1)} %fusion.19), channel_id=1, source_target_pairs={{0,8},{8,0},{16,24},{24,16},{1,9},{9,1},{17,25},{25,17},{2,10},{10... | collective-permute-start | bytes 1572872 | tf_op jit(solution)/shard_map/ppermute | solution.py:554
  235.5 56.0 %collective-permute-start.52 = (f32[2,1024,256]{2,1,0:T(8,128)S(1)}, f32[2,1024,256]{2,1,0:T(8,128)S(1)}, u32[]{:S(2)}, u32[]{:S(2)}) collective-permute-start(f32[2,1024,256]{2,1,0:T(8,128)S(1)} %copy-done.123), channel_id=1, source_target_pairs={{0,1},{1,0},{2,3},{3,2},{4,5},{5,4},{6,7},{7,6},{8,9},{9,8},{10,11... | collective-permute-start | bytes 6291464 | tf_op jit(solution)/shard_map/ppermute | solution.py:554
  238.1 36.4 %collective-permute-start.47 = (f32[256,1024]{1,0:T(8,128)S(1)}, f32[256,1024]{1,0:T(8,128)S(1)}, u32[]{:S(2)}, u32[]{:S(2)}) collective-permute-start(f32[256,1024]{1,0:T(8,128)S(1)} %fusion.6), channel_id=1, source_target_pairs={{0,8},{8,0},{16,24},{24,16},{1,9},{9,1},{17,25},{25,17},{2,10},{10... | collective-permute-start | bytes 3145736 | tf_op jit(solution)/shard_map/ppermute | solution.py:554
  250.5 26.3 %collective-permute-start.59 = (f32[1024,256]{1,0:T(8,128)S(1)}, f32[1024,256]{1,0:T(8,128)S(1)}, u32[]{:S(2)}, u32[]{:S(2)}) collective-permute-start(f32[1024,256]{1,0:T(8,128)S(1)} %fusion), channel_id=1, source_target_pairs={{0,16},{8,24},{16,0},{24,8},{1,17},{9,25},{17,1},{25,9},{2,18},{10... | collective-permute-start | bytes 3145736 | tf_op jit(solution)/shard_map/ppermute | solution.py:554
  269.4 24.9 %collective-permute-start.23 = (f32[256,512]{1,0:T(8,128)S(1)}, f32[256,512]{1,0:T(8,128)S(1)}, u32[]{:S(2)}, u32[]{:S(2)}) collective-permute-start(f32[256,512]{1,0:T(8,128)S(1)} %fusion.22), channel_id=1, source_target_pairs={{0,16},{8,24},{16,0},{24,8},{1,17},{9,25},{17,1},{25,9},{2,18},{10... | collective-permute-start | bytes 1572872 | tf_op jit(solution)/shard_map/ppermute | solution.py:554
  280.9 37.2 %collective-permute-start.17 = (f32[288,512]{1,0:T(8,128)S(1)}, f32[288,512]{1,0:T(8,128)S(1)}, u32[]{:S(2)}, u32[]{:S(2)}) collective-permute-start(f32[288,512]{1,0:T(8,128)S(1)} %fusion.13), channel_id=1, source_target_pairs={{0,8},{8,0},{16,24},{24,16},{1,9},{9,1},{17,25},{25,17},{2,10},{10... | collective-permute-start | bytes 1769480 | tf_op jit(solution)/shard_map/ppermute | solution.py:554
  287.0 39.6 %collective-permute-start.48 = (f32[128,1024]{1,0:T(8,128)S(1)}, f32[128,1024]{1,0:T(8,128)S(1)}, u32[]{:S(2)}, u32[]{:S(2)}) collective-permute-start(f32[128,1024]{1,0:T(8,128)S(1)} %slice.435), channel_id=1, source_target_pairs={{0,2},{1,3},{2,0},{3,1},{4,6},{5,7},{6,4},{7,5},{8,10},{9,11},{10,... | collective-permute-start | bytes 1572872 | tf_op jit(solution)/shard_map/ppermute | solution.py:554
  288.5 49.2 %collective-permute-start.60 = (f32[512,256]{1,0:T(8,128)S(1)}, f32[512,256]{1,0:T(8,128)S(1)}, u32[]{:S(2)}, u32[]{:S(2)}) collective-permute-start(f32[512,256]{1,0:T(8,128)S(1)} %slice.448), channel_id=1, source_target_pairs={{0,2},{1,3},{2,0},{3,1},{4,6},{5,7},{6,4},{7,5},{8,10},{9,11},{10,... | collective-permute-start | bytes 1572872 | tf_op jit(solution)/shard_map/ppermute | solution.py:554
  299.6 77.2 %collective-permute-start.41 = (f32[256,1024]{1,0:T(8,128)}, f32[256,1024]{1,0:T(8,128)}, u32[]{:S(2)}, u32[]{:S(2)}) collective-permute-start(f32[256,1024]{1,0:T(8,128)} %fusion.9), channel_id=1, source_target_pairs={{0,8},{8,0},{16,24},{24,16},{1,9},{9,1},{17,25},{25,17},{2,10},{10... | collective-permute-start | bytes 3145736 | tf_op jit(solution)/shard_map/ppermute | solution.py:554
  300.1 16.3 %collective-permute-start.24 = (f32[128,512]{1,0:T(8,128)S(1)}, f32[128,512]{1,0:T(8,128)S(1)}, u32[]{:S(2)}, u32[]{:S(2)}) collective-permute-start(f32[128,512]{1,0:T(8,128)S(1)} %slice.395), channel_id=1, source_target_pairs={{0,2},{1,3},{2,0},{3,1},{4,6},{5,7},{6,4},{7,5},{8,10},{9,11},{10,... | collective-permute-start | bytes 786440 | tf_op jit(solution)/shard_map/ppermute | solution.py:554
  316.4 62.9 %collective-permute-start.53 = (f32[1024,256]{1,0:T(8,128)}, f32[1024,256]{1,0:T(8,128)}, u32[]{:S(2)}, u32[]{:S(2)}) collective-permute-start(f32[1024,256]{1,0:T(8,128)} %fusion.3), channel_id=1, source_target_pairs={{0,16},{8,24},{16,0},{24,8},{1,17},{9,25},{17,1},{25,9},{2,18},{10... | collective-permute-start | bytes 3145736 | tf_op jit(solution)/shard_map/ppermute | solution.py:554
  326.6 12.1 %collective-permute-start.26 = (f32[64,512]{1,0:T(8,128)S(1)}, f32[64,512]{1,0:T(8,128)S(1)}, u32[]{:S(2)}, u32[]{:S(2)}) collective-permute-start(f32[64,512]{1,0:T(8,128)S(1)} %slice_add_fusion.29), channel_id=1, source_target_pairs={{0,8},{8,0},{16,24},{24,16},{1,9},{9,1},{17,25},{25,17},{2,10},{10... | collective-permute-start | bytes 393224 | tf_op jit(solution)/shard_map/ppermute | solution.py:554
  335.5 28.8 %collective-permute-start.49 = (f32[64,1024]{1,0:T(8,128)S(1)}, f32[64,1024]{1,0:T(8,128)S(1)}, u32[]{:S(2)}, u32[]{:S(2)}) collective-permute-start(f32[64,1024]{1,0:T(8,128)S(1)} %slice.437), channel_id=1, source_target_pairs={{0,4},{1,5},{2,6},{3,7},{4,0},{5,1},{6,2},{7,3},{8,12},{9,13},{10,... | collective-permute-start | bytes 786440 | tf_op jit(solution)/shard_map/ppermute | solution.py:554
  337.7 19.8 %collective-permute-start.19 = (f32[72,512]{1,0:T(8,128)S(1)}, f32[72,512]{1,0:T(8,128)S(1)}, u32[]{:S(2)}, u32[]{:S(2)}) collective-permute-start(f32[72,512]{1,0:T(8,128)S(1)} %slice.383), channel_id=1, source_target_pairs={{0,4},{1,5},{2,6},{3,7},{4,0},{5,1},{6,2},{7,3},{8,12},{9,13},{10,... | collective-permute-start | bytes 442376 | tf_op jit(solution)/shard_map/ppermute | solution.py:554
  338.7 28.4 %collective-permute-start.61 = (f32[256,256]{1,0:T(8,128)S(1)}, f32[256,256]{1,0:T(8,128)S(1)}, u32[]{:S(2)}, u32[]{:S(2)}) collective-permute-start(f32[256,256]{1,0:T(8,128)S(1)} %slice.450), channel_id=1, source_target_pairs={{0,4},{1,5},{2,6},{3,7},{4,0},{5,1},{6,2},{7,3},{8,12},{9,13},{10,... | collective-permute-start | bytes 786440 | tf_op jit(solution)/shard_map/ppermute | solution.py:554
  365.1 53.2 %collective-permute-start.50 = (f32[64,1024]{1,0:T(8,128)}, f32[64,1024]{1,0:T(8,128)}, u32[]{:S(2)}, u32[]{:S(2)}) collective-permute-start(f32[64,1024]{1,0:T(8,128)} %slice_add_fusion.21), channel_id=1, source_target_pairs={{0,16},{8,24},{16,0},{24,8},{1,17},{9,25},{17,1},{25,9},{2,18},{10... | collective-permute-start | bytes 786440 | tf_op jit(solution)/shard_map/ppermute | solution.py:554
  367.8 16.0 %collective-permute-start.62 = (f32[256,256]{1,0:T(8,128)}, f32[256,256]{1,0:T(8,128)}, u32[]{:S(2)}, u32[]{:S(2)}) collective-permute-start(f32[256,256]{1,0:T(8,128)} %slice_add_fusion.19), channel_id=1, source_target_pairs={{0,8},{8,0},{16,24},{24,16},{1,9},{9,1},{17,25},{25,17},{2,10},{10... | collective-permute-start | bytes 786440 | tf_op jit(solution)/shard_map/ppermute | solution.py:554
  379.2 16.6 %collective-permute-start.42 = (f32[128,1024]{1,0:T(8,128)S(1)}, f32[128,1024]{1,0:T(8,128)S(1)}, u32[]{:S(2)}, u32[]{:S(2)}) collective-permute-start(f32[128,1024]{1,0:T(8,128)S(1)} %slice.429), channel_id=1, source_target_pairs={{0,2},{1,3},{2,0},{3,1},{4,6},{5,7},{6,4},{7,5},{8,10},{9,11},{10,... | collective-permute-start | bytes 1572872 | tf_op jit(solution)/shard_map/ppermute | solution.py:554
  380.8 21.6 %collective-permute-start.54 = (f32[512,256]{1,0:T(8,128)S(1)}, f32[512,256]{1,0:T(8,128)S(1)}, u32[]{:S(2)}, u32[]{:S(2)}) collective-permute-start(f32[512,256]{1,0:T(8,128)S(1)} %slice.442), channel_id=1, source_target_pairs={{0,2},{1,3},{2,0},{3,1},{4,6},{5,7},{6,4},{7,5},{8,10},{9,11},{10,... | collective-permute-start | bytes 1572872 | tf_op jit(solution)/shard_map/ppermute | solution.py:554
  384.9 37.6 %collective-permute-start.63 = (f32[256,256]{1,0:T(8,128)S(1)}, f32[256,256]{1,0:T(8,128)}, u32[]{:S(2)}, u32[]{:S(2)}) collective-permute-start(f32[256,256]{1,0:T(8,128)S(1)} %add.406), channel_id=1, source_target_pairs={{0,16},{8,24},{16,0},{24,8},{1,17},{9,25},{17,1},{25,9},{2,18},{10... | collective-permute-start | bytes 786440 | tf_op jit(solution)/shard_map/ppermute | solution.py:554
  395.9 19.6 %collective-permute-start.43 = (f32[64,1024]{1,0:T(8,128)S(1)}, f32[64,1024]{1,0:T(8,128)S(1)}, u32[]{:S(2)}, u32[]{:S(2)}) collective-permute-start(f32[64,1024]{1,0:T(8,128)S(1)} %slice.431), channel_id=1, source_target_pairs={{0,4},{1,5},{2,6},{3,7},{4,0},{5,1},{6,2},{7,3},{8,12},{9,13},{10,... | collective-permute-start | bytes 786440 | tf_op jit(solution)/shard_map/ppermute | solution.py:554
  402.5 17.3 %collective-permute-start.55 = (f32[256,256]{1,0:T(8,128)S(1)}, f32[256,256]{1,0:T(8,128)S(1)}, u32[]{:S(2)}, u32[]{:S(2)}) collective-permute-start(f32[256,256]{1,0:T(8,128)S(1)} %slice.444), channel_id=1, source_target_pairs={{0,4},{1,5},{2,6},{3,7},{4,0},{5,1},{6,2},{7,3},{8,12},{9,13},{10,... | collective-permute-start | bytes 786440 | tf_op jit(solution)/shard_map/ppermute | solution.py:554
  (197 other events, 1491.0 us)

commit v2 on v1

--- a/solution.py
+++ b/solution.py
@@ -185,7 +185,7 @@
 
 
 def front_body(meta, starts, hidden, gain, shift, w, b, tables, dct, outs):
-    first_ref, second_ref, fq_ref, fk_ref, v_ref, eq_ref, ek_ref, keep_ref, send_ref = outs
+    first_ref, second_ref, fq_ref, fk_ref, v_ref, eq_ref, ek_ref, keep_ref, send_ref, *_ = outs
     xhat, _ = norm_parts(hidden)
     gains, shifts = gain[...].astype(f32), shift[...].astype(f32)
     first = (xhat * gains[0:1] + shifts[0:1]).astype(bf16)
@@ -222,8 +222,11 @@
     fq_ref[...] = exp_q.astype(bf16)
 
 
-def front_kernel(meta, starts, h, gain, shift, w, b, ta, tb, tc, dh, dl, *outs):
+def front_kernel(meta, starts, h, cot, gain, shift, w, b, ta, tb, tc, dh, dl, *outs):
     front_body(meta, starts, h[...].astype(f32), gain, shift, w, b, (ta, tb, tc), (dh, dl), outs)
+    early = outs[9]
+    early[0] = outs[1][...].astype(f32)
+    early[1] = cot[...].astype(f32)
 
 
 def attend(meta, starts, num_ref, kt_ref, fq_ref, mine_ref, theirs_ref, den_ref, att_ref, low_ref):
@@ -254,6 +257,12 @@
     hidden = h[...].astype(f32) + (dot(att_low[...], ow[...]) + ob[...].astype(f32)) + feed[...]
     h2[...] = hidden
     front_body(meta, starts, hidden, gain, shift, w, b, (ta, tb, tc), (dh, dl), outs)
+    store_rows(outs[1], outs[9:])
+
+
+def store_rows(x, refs):
+    for row, ref in enumerate(refs):
+        ref[...] = x[row * LEN : (row + 1) * LEN].astype(f32)
 
 
 def attend_back(meta, starts, up, ow, den, att, fq, gnum, gden, keep_ref, send_ref):
@@ -410,7 +419,7 @@
 def turn_back_kernel(
     meta, starts, mine, theirs, gfq, gfk, gval, fk, v, eq, ek, ta, tb, tc, dh, dl, w, h, gain, gsecond, cot,
     ow, den, att, fq,
-    gp, gqb, ggain, gshift, up_ref, up_low, gnum, gden, keep, send, gob,
+    gp, gqb, ggain, gshift, up_ref, up_low, gnum, gden, keep, send, gob, *up_rows,
 ):
     packed_back(
         meta, starts, mine, theirs, gfq, gfk, gval, fk, v, eq, ek, (ta, tb, tc), (dh, dl), gp, gqb
@@ -420,6 +429,7 @@
     up_ref[...] = up
     low = up.astype(bf16)
     up_low[...] = low
+    store_rows(up_low, up_rows)
     attend_back(meta, starts, low, ow, den, att, fq, gnum, gden, keep, send)
     gob[...] = jnp.sum(low.astype(f32), axis=0, keepdims=True)
 
@@ -453,21 +463,76 @@
     return held[...].astype(bf16)
 
 
-def feed_grad_kernel(size, meta, second, act, lift, up, in_keep, in_send, down_keep, down_send, f1, h1, f2, h2):
-    left = gathered(size, meta, second[...], f1, h1)
-    for k in range(2):
-        for g in range(2):
-            at = pl.multiple_of((k ^ meta[3]) * (FF // 2) + g * WIDE, WIDE)
-            out = dot(left, lift[:, pl.ds(at, WIDE)])
-            in_keep[k, :, g * WIDE : (g + 1) * WIDE] = out[: D // 2]
-            in_send[k, :, g * WIDE : (g + 1) * WIDE] = out[D // 2 :]
-    left = gathered(size, meta, act[...], f2, h2)
-    for k in range(2):
-        right = up[:, pl.ds(pl.multiple_of((k ^ meta[4]) * (D // 2), D // 2), D // 2)]
-        for g in range(4):
-            out = dot(left[g * WIDE : (g + 1) * WIDE], right)
-            ref = (down_keep, down_send)[g // 2]
-            ref[k, (g % 2) * WIDE : (g % 2 + 1) * WIDE, :] = out
+def feed_grad_kernel(size, early_is_second, meta, *refs):
+    *sources, iw, ib, dw, keep, send, s_all, u_all, act, lift, out = refs
+    load_tokens(meta, early_is_second, sources, s_all, u_all)
+    tokens = s_all.shape[0] // 4
+    for k in range(4):
+        at = slice(k * tokens, (k + 1) * tokens)
+        lifted = dot(s_all[at], iw[...]) + ib[...].astype(f32)
+        value, slope = gelu_parts(lifted)
+        act[at] = value.astype(bf16)
+        lift[at] = (dot(u_all[at], dw[...], NT) * slope).astype(bf16)
+    block = D // size
+    count = size.bit_length() - 1
+    for part, grads in enumerate(
+        (dot(s_all[...], lift[...], TN), dot(act[...], u_all[...], TN))
+    ):
+        for s in range(size):
+            place = reversed_bits(s ^ meta[2], count)
+            at = pl.multiple_of((2 * place + part) * block, block)
+            out[pl.ds(at, block), :] = grads[s * block : (s + 1) * block]
+    half = out.shape[0] // 2
+    keep[...] = out[:half]
+    send[...] = out[half:]
+
+
+def load_tokens(meta, early_is_second, sources, s_all, u_all):
+    early_ref, own0, own1, a1, a2, b1, b2 = sources
+    fresh, early = (u_all, s_all) if early_is_second else (s_all, u_all)
+    tokens = s_all.shape[0] // 4
+    for k in range(4):
+        early[k * tokens : (k + 1) * tokens] = early_ref[
+            k ^ meta[5], 0 if early_is_second else 1
+        ].astype(bf16)
+    half = tokens // 2
+    places = (own0[...], own1[...], a1[...], b2[:half], a2[:half], b1[...], a2[half:], b2[half:])
+    for k, value in enumerate(places):
+        fresh[k * half : (k + 1) * half] = value.astype(bf16)
+
+
+def chosen(refs, index):
+    value = refs[0][...]
+    for k in range(1, len(refs)):
+        value = jnp.where(index == k, refs[k][...], value)
+    return value
+
+
+def join_kernel(meta, *refs):
+    pieces, outs = refs[:-4], refs[-4:]
+    in_out, down_out, qkv_out, out_out = outs
+    block = in_out.shape[1]
+    low = low_lanes(block)
+    for layer in range(2):
+        own, first, rest, a_own, a_other, b_own, b_other = pieces[7 * layer : 7 * layer + 7]
+        both = (rest.at[: 2 * block], rest.at[2 * block :])
+        held = (own, first, *both) if layer == 1 else (own, both[0], first, both[1])
+        for pair in range(2):
+            left, right = (chosen(held, q ^ meta[5]) for q in (2 * pair, 2 * pair + 1))
+            down_out[layer, 2 * pair * block : (2 * pair + 1) * block, :] = left[block:]
+            down_out[layer, (2 * pair + 1) * block : (2 * pair + 2) * block, :] = right[block:]
+            for tile in range(D // 128):
+                lanes = slice(tile * 128, (tile + 1) * 128)
+                a, b = left[:block, lanes], right[:block, lanes]
+                at = 2 * tile * 256 + pair * 128
+                in_out[layer, :, at : at + 128] = jnp.where(low, a, pltpu.roll(b, 64, 1))
+                in_out[layer, :, at + 256 : at + 384] = jnp.where(low, pltpu.roll(a, 64, 1), b)
+        for part, (mine, other) in enumerate(((a_own, a_other), (b_own, b_other))):
+            for k in range(2):
+                value = jnp.where(meta[3 + part] == k, mine[:block], other[:block])
+                q = 2 * part + k
+                qkv_out[layer, :, q * 384 : (q + 1) * 384] = value[:, :384]
+                out_out[layer, :, q * 128 : (q + 1) * 128] = value[:, 384:]
 
 
 def packed_grad_kernel(size, meta, first, att_low, gp, up, a_keep, a_send, b_keep, b_send, f1, h1):
@@ -521,7 +586,7 @@
         out_shape=list(outs),
         scratch_shapes=list(scratch),
         cost_estimate=pl.CostEstimate(flops=int(flops), bytes_accessed=moved, transcendentals=0),
-        compiler_params=pltpu.CompilerParams(vmem_limit_bytes=40 * 1024 * 1024),
+        compiler_params=pltpu.CompilerParams(vmem_limit_bytes=62 * 1024 * 1024),
     )(*arrays)
 
 
@@ -554,31 +619,38 @@
     return lax.ppermute(value, axis, [(i, i ^ bit) for i in range(size)])
 
 
-def chips_on(value, step):
-    size = lax.axis_size("seq")
-    pairs = [(i, i + 2 * step) for i in range(size) if 0 <= i + 2 * step < size]
-    return lax.ppermute(value, "seq", pairs)
-
-
-def exchange(keep, send, flag, core, chip, backward):
+def tie(*values):
+    return lax.optimization_barrier(values)
+
+
+def exchange(keep, send, flag, core, chip, backward, works=()):
     chips = lax.axis_size("seq") // 2
     begin, span = chip * 2 * LEN, 2 * LEN
     got = flip(send, "seq", 1)
     even, odd = jnp.where(core == 0, keep, got), jnp.where(core == 0, got, keep)
-    sign = -1 if backward else 1
     if backward:
-        whole = even + flag(begin + LEN - 1, begin) * odd
+        total = even + flag(begin + LEN - 1, begin) * odd
     else:
-        whole = odd + flag(begin + span - 1, begin + LEN) * even
-    entered = chips_on(whole, sign)
-    step = 2
+        total = odd + flag(begin + span - 1, begin + LEN) * even
+    entered, made, step = None, [], 1
     while step < chips:
-        partial = whole + flag(begin + span - 1, begin) * entered
-        more = chips_on(partial, sign * step)
+        other = flip(total, "seq", 2 * step)
+        if len(made) < len(works):
+            found = works[len(made)](lambda x, total=total: tie(total, x)[1])
+            leaves, tree = jax.tree.flatten(found)
+            other, *leaves = tie(other, *leaves)
+            made.append(jax.tree.unflatten(tree, leaves))
+        upper = (chip // step) % 2 == 1
+        first = chip - chip % (2 * step)
+        middle = first + step
+        later, earlier = jnp.where(upper, total, other), jnp.where(upper, other, total)
         if backward:
-            entered = entered + flag(begin + span * step - 1, begin + span) * more
+            passed = jnp.where(upper, 0.0, flag(middle * span - 1, (chip + 1) * span))
+            total = earlier + flag(middle * span - 1, first * span) * later
         else:
-            entered = entered + flag(begin - 1, begin - span * (step - 1)) * more
+            passed = jnp.where(upper, flag(chip * span - 1, middle * span), 0.0)
+            total = later + flag((middle + step) * span - 1, middle * span) * earlier
+        entered = passed * other if entered is None else entered + passed * other
         step *= 2
     if backward:
         for_even, for_odd = odd + flag(begin + span - 1, begin + LEN) * entered, entered
@@ -586,21 +658,51 @@
         for_even, for_odd = entered, even + flag(begin + LEN - 1, begin) * entered
     mine = jnp.where(core == 0, for_even, for_odd)
     theirs = flip(jnp.where(core == 0, for_odd, for_even), "seq", 1)
-    return mine, theirs
-
-
-def reduce_chunk(keep, send, bit):
-    size = lax.axis_size("seq")
-    got = flip(send, "seq", 1)
-    got_first = flip(keep[1] + got[1], "batch", bit)
-    total = keep[0] + got[0] + got_first
+    return (mine, theirs), made
+
+
+def halved(total):
     step = 2
-    while step < size:
+    while step < lax.axis_size("seq"):
         half = total.shape[0] // 2
         total = total[:half] + flip(total[half:], "seq", step)
         step *= 2
+    return total
+
+
+def reduce_chunk(keep, send, bit):
+    got = flip(send, "seq", 1)
+    got_first = flip(keep[1] + got[1], "batch", bit)
+    total = halved(keep[0] + got[0] + got_first)
     total = total + flip(total, "batch", 3 - bit)
     return total, flip(total, "batch", bit)
+
+
+def reduce_quarter(keep, send, bit):
+    total = halved(keep + flip(send, "seq", 1))
+    other = flip(total, "batch", bit)
+    return total, other, flip(jnp.concatenate([total, other], axis=0), "batch", 3 - bit)
+
+
+def join(pieces, column, bits, size):
+    slot = D // size
+    made = [[], [], [], []]
+    for layer in range(2):
+        own, first, rest, a_own, a_other, b_own, b_other = pieces[7 * layer : 7 * layer + 7]
+        both = (rest[: 2 * slot], rest[2 * slot :])
+        held = (own, first, *both) if layer == 1 else (own, both[0], first, both[1])
+        held = jnp.take(jnp.stack(held), np.arange(4) ^ column, axis=0)
+        made[0].append(
+            held[:, :slot].reshape(4, slot, size, slot).transpose(1, 2, 0, 3).reshape(slot, FF)
+        )
+        made[1].append(held[:, slot:].reshape(4 * slot, D))
+        quarters = []
+        for bit, mine, other in ((bits[0], a_own, a_other), (bits[1], b_own, b_other)):
+            mine, other = mine[:slot], other[:slot]
+            quarters += [jnp.where(bit == 0, mine, other), jnp.where(bit == 0, other, mine)]
+        made[2].append(jnp.concatenate([q[:, :384] for q in quarters], axis=1))
+        made[3].append(jnp.concatenate([q[:, 384:] for q in quarters], axis=1))
+    return [jnp.stack(part) for part in made]
 
 
 def per_device(
@@ -639,7 +741,7 @@
     )
     tables = rotary_tables((absolute[None, :] - segment).reshape(tokens))
     dct = cosine_table()
-    meta = Scalars(jnp.stack([begin, core, me, bits[0], bits[1]]).astype(jnp.int32))
+    meta = Scalars(jnp.stack([begin, core, me, bits[0], bits[1], column]).astype(jnp.int32))
     starts = Scalars(doc_starts)
     hidden0 = inputs.reshape(tokens, D)
     cot = cotangent.reshape(tokens, D)
@@ -664,102 +766,40 @@
             *dct,
         ]
 
-    first, second, fq, fk, v, eq, ek, keep, send = call(
-        front_kernel, "front", [meta, starts, hidden0, *front_of(0)], front_outs, 6 * matmul
-    )
-    entered0 = exchange(keep, send, flag, core, chip, False)
+    quarter_wide = FF // size // 4
     feed_weights = [
         [Layer(x, layer) for x in (in_weight, in_bias2, down_weight, down_bias2)]
         for layer in range(2)
     ]
-    act0, slope0, feed0 = call(
-        feed_kernel,
-        "feed",
-        [second, *feed_weights[0]],
-        [sds((tokens, FF), bf16), sds((tokens, FF)), tall],
-        8 * matmul,
-    )
-    intra_outs = [sds((rows, PAIRS, 2 * LEN, LEN), bf16), tall, tall]
-    scores0, num0, kt0 = call(
-        intra_kernel, "intra", [meta, starts, fq, fk, v], intra_outs, 2 * matmul
-    )
-    first0, second0, fq0, fk0, v0, eq0, ek0 = first, second, fq, fk, v, eq, ek
-    den0, att0, att_low0, hidden1, first1, second1, fq1, fk1, v1, eq1, ek1, keep, send = call(
-        middle_kernel,
-        "middle",
-        [meta, starts, hidden0, feed0, num0, kt0, fq0, *entered0]
-        + [Layer(out_weight, 0), Layer(out_bias2, 0), *front_of(1)],
-        [tall, tall, fat, tall] + front_outs,
-        8 * matmul,
-    )
-    entered1 = exchange(keep, send, flag, core, chip, False)
-    act1, feed1, lift1, gsecond1, gib1 = call(
-        feed_both_kernel,
-        "feed_both",
-        [second1, *feed_weights[1], cot],
-        [sds((tokens, FF), bf16), tall, sds((tokens, FF), bf16), tall, sds((1, FF))],
-        16 * matmul,
-    )
-    scores1, num1, kt1 = call(
-        intra_kernel, "intra", [meta, starts, fq1, fk1, v1], intra_outs, 2 * matmul
-    )
-
-    def feed_grad(second, act, lift, up):
-        wide, narrow = sds((2, D // 2, FF // 2)), sds((2, FF // 2, D // 2))
-        flat = [pltpu.VMEM((D, tokens), f32)] * 2 + [pltpu.VMEM((FF, tokens), f32)] * 2
-        a_keep, a_send, b_keep, b_send = call(
-            functools.partial(feed_grad_kernel, size),
+
+    def quarter_weights(layer):
+        shape = (size, 4, quarter_wide)
+        pick = functools.partial(lax.dynamic_index_in_dim, index=column, keepdims=False)
+        return [
+            pick(in_weight[layer].reshape((D,) + shape), axis=2).reshape(D, D),
+            pick(in_bias[layer].reshape(shape), axis=1).reshape(1, D),
+            pick(down_weight[layer].reshape(shape + (D,)), axis=1).reshape(D, D),
+        ]
+
+    def gather_first(rows):
+        return flip(rows[0], "batch", 1), flip(rows[1], "batch", 2)
+
+    def gather_second(rows, firsts):
+        a = jnp.concatenate([rows[0], firsts[0]], axis=0)
+        b = jnp.concatenate([rows[1], firsts[1]], axis=0)
+        return flip(a, "batch", 2), flip(b, "batch", 1)
+
+    def feed_grad(early, fresh, firsts, seconds, layer):
+        halves = [sds((D, D))] * 2
+        operands = [early, *fresh, firsts[0], seconds[0], firsts[1], seconds[1]]
+        return call(
+            functools.partial(feed_grad_kernel, size, layer == 0),
             "feed_grad",
-            [meta, second, act, lift, up],
-            [wide, wide, narrow, narrow],
-            8 * matmul,
-            flat,
+            [meta, *operands, *quarter_weights(layer)],
+            halves,
+            16 * matmul,
+            [pltpu.VMEM((4 * tokens, D), bf16)] * 4 + [pltpu.VMEM((2 * D, D), f32)],
         )
-        return reduce_chunk(a_keep, a_send, 1), reduce_chunk(b_keep, b_send, 2)
-
-    chunk_feed1 = feed_grad(second1, act1, lift1, cot)
-    den1, att1, att_low1, result, gnum1, gden1, keep, send, gob1 = call(
-        turn_kernel,
-        "turn",
-        [meta, starts, hidden1, feed1, num1, kt1, fq1, *entered1]
-        + [Layer(out_weight, 1), Layer(out_bias2, 1), cot],
-        [tall, tall, fat, fat, fat, tall, packed_state, packed_state, sds((1, D))],
-        3 * matmul,
-    )
-    later1 = exchange(keep, send, flag, core, chip, True)
-    gfq1, gfk1, gval1 = call(
-        intra_back_kernel,
-        "intra_back",
-        [meta, starts, fq1, fk1, v1, scores1, gnum1, gden1, *entered1],
-        [tall, tall, tall],
-        4 * matmul,
-    )
-    vector_outs = [sds((1, 3 * D)), sds((2, D)), sds((2, D))]
-    packed = sds((tokens, 3 * D), bf16)
-    gp1, gqb1, ggain1, gshift1, up0, up_low0, gnum0, gden0, keep, send, gob0 = call(
-        turn_back_kernel,
-        "turn_back",
-        [meta, starts, *later1, gfq1, gfk1, gval1, fk1, v1, eq1, ek1, *tables, *dct]
-        + [Layer(qkv_weight, 1), hidden1, Layer(norm_gain, 1), gsecond1, cot]
-        + [Layer(out_weight, 0), den0, att0, fq0],
-        [packed, *vector_outs, tall, fat, fat, tall, packed_state, packed_state, sds((1, D))],
-        8 * matmul,
-    )
-    later0 = exchange(keep, send, flag, core, chip, True)
-    lift0, gsecond0, gib0 = call(
-        feed_back_kernel,
-        "feed_back",
-        [slope0, up_low0, Layer(in_weight, 0), Layer(down_weight, 0)],
-        [sds((tokens, FF), bf16), tall, sds((1, FF))],
-        8 * matmul,
-    )
-    gfq0, gfk0, gval0 = call(
-        intra_back_kernel,
-        "intra_back",
-        [meta, starts, fq0, fk0, v0, scores0, gnum0, gden0, *entered0],
-        [tall, tall, tall],
-        4 * matmul,
-    )
 
     def packed_grad(first, att_low, gp, up):
         quarter = sds((2, D // 2, D))
@@ -773,9 +813,116 @@
             flat,
         )
 
+    line = sds((LEN, D))
+    first0, second0, fq0, fk0, v0, eq0, ek0, keep, send, early = call(
+        front_kernel,
+        "front",
+        [meta, starts, hidden0, cot, *front_of(0)],
+        front_outs + [sds((2, tokens, D))],
+        6 * matmul,
+    )
+    early = lax.all_gather(early, "batch")
+    intra_outs = [sds((rows, PAIRS, 2 * LEN, LEN), bf16), tall, tall]
+
+    def do_feed(gate):
+        return call(
+            feed_kernel,
+            "feed",
+            [gate(second0), *feed_weights[0]],
+            [sds((tokens, FF), bf16), sds((tokens, FF)), tall],
+            8 * matmul,
+        )
+
+    def do_intra(fq, fk, v):
+        return lambda gate: call(
+            intra_kernel, "intra", [meta, starts, gate(fq), fk, v], intra_outs, 2 * matmul
+        )
+
+    entered0, made = exchange(
+        keep, send, flag, core, chip, False, [do_feed, do_intra(fq0, fk0, v0)]
+    )
+    (_, slope0, feed0), (scores0, num0, kt0) = made
+    (
+        den0, att0, att_low0, hidden1, first1, second1, fq1, fk1, v1, eq1, ek1, keep, send, *rows1
+    ) = call(
+        middle_kernel,
+        "middle",
+        [meta, starts, hidden0, feed0, num0, kt0, fq0, *entered0]
+        + [Layer(out_weight, 0), Layer(out_bias2, 0), *front_of(1)],
+        [tall, tall, fat, tall] + front_outs + [line] * 2,
+        8 * matmul,
+    )
+
+    def do_feed_both(gate):
+        return gather_first([gate(row) for row in rows1]), call(
+            feed_both_kernel,
+            "feed_both",
+            [gate(second1), *feed_weights[1], cot],
+            [sds((tokens, FF), bf16), tall, sds((tokens, FF), bf16), tall, sds((1, FF))],
+            16 * matmul,
+        )
+
+    entered1, made = exchange(
+        keep, send, flag, core, chip, False, [do_feed_both, do_intra(fq1, fk1, v1)]
+    )
+    (firsts1, (_, feed1, _, gsecond1, gib1)), (scores1, num1, kt1) = made
+    seconds1 = gather_second(rows1, firsts1)
+    den1, att1, att_low1, result, gnum1, gden1, keep, send, gob1 = call(
+        turn_kernel,
+        "turn",
+        [meta, starts, hidden1, feed1, num1, kt1, fq1, *entered1]
+        + [Layer(out_weight, 1), Layer(out_bias2, 1), cot],
+        [tall, tall, fat, fat, fat, tall, packed_state, packed_state, sds((1, D))],
+        3 * matmul,
+    )
+
+    def do_intra_back(fq, fk, v, scores, gnum, gden, entered):
+        return lambda gate: call(
+            intra_back_kernel,
+            "intra_back",
+            [meta, starts, gate(fq), fk, v, scores, gnum, gden, *entered],
+            [tall, tall, tall],
+            4 * matmul,
+        )
+
+    later1, made = exchange(
+        keep, send, flag, core, chip, True,
+        [do_intra_back(fq1, fk1, v1, scores1, gnum1, gden1, entered1)],
+    )
+    ((gfq1, gfk1, gval1),) = made
+    vector_outs = [sds((1, 3 * D)), sds((2, D)), sds((2, D))]
+    packed = sds((tokens, 3 * D), bf16)
+    gp1, gqb1, ggain1, gshift1, up0, up_low0, gnum0, gden0, keep, send, gob0, *rows0 = call(
+        turn_back_kernel,
+        "turn_back",
+        [meta, starts, *later1, gfq1, gfk1, gval1, fk1, v1, eq1, ek1, *tables, *dct]
+        + [Layer(qkv_weight, 1), hidden1, Layer(norm_gain, 1), gsecond1, cot]
+        + [Layer(out_weight, 0), den0, att0, fq0],
+        [packed, *vector_outs, tall, fat, fat, tall, packed_state, packed_state, sds((1, D))]
+        + [line] * 2,
+        8 * matmul,
+    )
+    feed_keep1, feed_send1 = feed_grad(early, rows1, firsts1, seconds1, 1)
+    chunk_feed1 = reduce_quarter(feed_keep1, feed_send1, 1)
+
+    def do_feed_back(gate):
+        firsts = gather_first([gate(row) for row in rows0])
+        return firsts, call(
+            feed_back_kernel,
+            "feed_back",
+            [slope0, gate(up_low0), Layer(in_weight, 0), Layer(down_weight, 0)],
+            [sds((tokens, FF), bf16), tall, sds((1, FF))],
+            8 * matmul,
+        )
+
+    later0, made = exchange(
+        keep, send, flag, core, chip, True,
+        [do_feed_back, do_intra_back(fq0, fk0, v0, scores0, gnum0, gden0, entered0)],
+    )
+    (firsts0, (_, gsecond0, gib0)), (gfq0, gfk0, gval0) = made
+    seconds0 = gather_second(rows0, firsts0)
     a_keep, a_send, b_keep, b_send = packed_grad(first1, att_low1, gp1, cot)
     chunk_packed1 = reduce_chunk(a_keep, a_send, 1), reduce_chunk(b_keep, b_send, 2)
-    chunk_feed0 = feed_grad(second0, act0, lift0, up_low0)
     gp0, gqb0, ggain0, gshift0, ginputs = call(
         last_kernel,
         "last",
@@ -785,80 +932,69 @@
         6 * matmul,
     )
     a_keep, a_send, b_keep, b_send = packed_grad(first0, att_low0, gp0, up_low0)
-
-    slot = D // size
-    vectors = jnp.concatenate(
-        [
-            part.reshape(-1, size, slot)
-            if part.shape[-1] != FF
-            else part.reshape(size, FF // D, slot).swapaxes(0, 1)
-            for layer in (
-                (ggain0, gshift0, gqb0.reshape(3, D), gob0, gib0),
-                (ggain1, gshift1, gqb1.reshape(3, D), gob1, gib1),
-            )
-            for part in layer
-        ],
-        axis=0,
-    ).swapaxes(0, 1)
-    count = size.bit_length() - 1
+    feed_keep0, feed_send0 = feed_grad(early, rows0, firsts0, seconds0, 0)
+    chunk_feed0 = reduce_quarter(feed_keep0, feed_send0, 2)
+
+    slot, count = D // size, size.bit_length() - 1
     order = np.array([reversed_bits(k, count) for k in range(size)], np.int32) ^ me
-    vectors = jnp.take(vectors, order, axis=0).reshape(size, 2, -1)
-    vectors = jnp.where(bits[0] == 0, vectors, vectors[:, ::-1]).swapaxes(0, 1)
-    held = vectors.shape[2]
-    under = -(-held // (8 * D)) * 8
-    vectors = jnp.pad(vectors, ((0, 0), (0, 0), (0, under * D - held)))
-    vectors = vectors.reshape(2, size, under, D)
-
-    def with_vectors(part, lines):
+
+    def lines_of(gain, shift, qkv_b, out_b, in_b):
+        vectors = jnp.concatenate([gain, shift, qkv_b.reshape(3, D), out_b], axis=0)
+        vectors = vectors.reshape(8, size, slot).swapaxes(0, 1)
+        wide = in_b.reshape(size, 4, slot)
+        wide = jnp.pad(wide, ((0, 0), (0, 4), (0, 0)))
+        lines = jnp.concatenate([vectors, wide], axis=2)
+        return jnp.pad(lines, ((0, 0), (0, 0), (0, D - 2 * slot)))
+
+    lines0 = lines_of(ggain0, gshift0, gqb0, gob0, gib0)
+    lines1 = lines_of(ggain1, gshift1, gqb1, gob1, gib1)
+    lines = jnp.where(
+        bits[0] == 0, jnp.stack([lines0, lines1]), jnp.stack([lines1, lines0])
+    )
+    lines = jnp.take(lines, order, axis=1)
+
+    def with_lines(part, lines):
         part = part.reshape(2, size // 2, slot, D)
         return jnp.concatenate([part, lines], axis=2).reshape(2, -1, D)
 
-    a_keep = with_vectors(a_keep, vectors[:, : size // 2])
-    a_send = with_vectors(a_send, vectors[:, size // 2 :])
-    own, other = reduce_chunk(a_keep, a_send, 1)
-    chunk_packed0 = (own[:slot], other[:slot]), reduce_chunk(b_keep, b_send, 2)
-    lines = [part[slot:].reshape(-1)[:held] for part in (own, other)]
-    summed = jnp.where(
-        bits[0] == 0, jnp.concatenate(lines), jnp.concatenate(lines[::-1])
-    ).reshape(2, 12, slot)
-
-    def joined(chunk, bit):
-        own, other = chunk
-        return jnp.where(
-            bit == 0,
-            jnp.concatenate([own, other], axis=-1),
-            jnp.concatenate([other, own], axis=-1),
+    a_keep = with_lines(a_keep, lines[:, : size // 2])
+    a_send = with_lines(a_send, lines[:, size // 2 :])
+    chunk_packed0 = reduce_chunk(a_keep, a_send, 1), reduce_chunk(b_keep, b_send, 2)
+    own, other = (part[slot:] for part in chunk_packed0[0])
+    summed = jnp.where(bits[0] == 0, jnp.stack([own, other]), jnp.stack([other, own]))
+    grad_in_b = summed[:, :4, slot : 2 * slot].reshape(2, FF // size)
+    summed = summed[:, :, :slot]
+    grad_out_b = summed[:, 7]
+
+    pieces = [
+        piece
+        for feed, (a, b) in ((chunk_feed0, chunk_packed0), (chunk_feed1, chunk_packed1))
+        for piece in (*feed, *a, *b)
+    ]
+    outs = [
+        sds((2, slot, FF)),
+        sds((2, FF // size, D)),
+        sds((2, slot, 3 * D)),
+        sds((2, slot, D)),
+    ]
+    if quarter_wide == HEAD:
+        grad_in, grad_down, grad_qkv, grad_out = call(
+            join_kernel, "join", [meta, *pieces], outs, matmul
         )
-
-    def of_layers(make):
-        return jnp.stack([make(0), make(1)])
-
-    chunks_feed, chunks_packed = (chunk_feed0, chunk_feed1), (chunk_packed0, chunk_packed1)
-
-    def columns(layer, begin, wide):
-        pieces = []
-        for part in range(2):
-            own, other = chunks_packed[layer][part]
-            pieces.append(
-                joined((own[:, begin : begin + wide], other[:, begin : begin + wide]), bits[part])
-            )
-        return jnp.concatenate(pieces, axis=-1)
-
-    grad_gain, grad_shift = summed[:, 0:2], summed[:, 2:4]
-    grad_qkv_b, grad_out_b = summed[:, 4:7], summed[:, 7]
-    grad_in_b = summed[:, 8:12].reshape(2, FF // size)
+    else:
+        grad_in, grad_down, grad_qkv, grad_out = join(pieces, column, bits, size)
     return (
         result.reshape(rows, length, D),
         ginputs.reshape(rows, length, D),
-        grad_gain,
-        grad_shift,
-        of_layers(lambda layer: columns(layer, 0, 384)),
-        grad_qkv_b,
-        of_layers(lambda layer: columns(layer, 384, 128)),
+        summed[:, 0:2],
+        summed[:, 2:4],
+        grad_qkv,
+        summed[:, 4:7],
+        grad_out,
         grad_out_b,
-        of_layers(lambda layer: joined(chunks_feed[layer][0], bits[0])),
+        grad_in,
         grad_in_b,
-        of_layers(lambda layer: joined(chunks_feed[layer][1], bits[1])),
+        grad_down,
         grad_out_b,
     )
 

time: 448 us -> 349 us (0.78)
  waiting for transfers between devices: 166 us -> 105 us
  local copies, waits for them, and re-layouts: 93.7 us -> 38 us
  Pallas kernels: 41.4 us -> 93.3 us
  starting transfers between devices: 82.5 us -> 56.8 us
  other arithmetic: 52.6 us -> 34.3 us
  between operations: 3.1 us -> 15.2 us
    unnamed x338 -> x105, local copies, waits for them, and re-layouts: 74.5 us -> 12.6 us
    pallas_call x16 -> x17, Pallas kernels: 41.4 us -> 93.3 us  [call(): pl.pallas_call(kernel, name=name, grid=(1,), in_specs=specs, out_specs=[p...]
    ppermute x56 -> x58, waiting for transfers between devices: 138 us -> 105 us  [flip(): return lax.ppermute(value, axis, [(i, i ^ bit) for i in range(size)])]
    ppermute x8 -> x0, waiting for transfers between devices: 28.3 us -> none  [chips_on(): return lax.ppermute(value, 'seq', pairs)]
    ppermute x8 -> x0, starting transfers between devices: 27.3 us -> none  [chips_on(): return lax.ppermute(value, 'seq', pairs)]
    slice x39 -> x20, local copies, waits for them, and re-layouts: 1.09 us -> 8.92 us  [the longest x1 5.02 us: quarter_weights(): in_weight[layer].reshape((D,) + shape)]
    reshape x13 -> x7, local copies, waits for them, and re-layouts: 11.5 us -> 4.2 us  [the longest x2 2.06 us: quarter_weights(): pick(in_weight[layer].reshape((D,) + shape), axis=2).reshape(D, D)]
    pallas_call x6 -> x4, other arithmetic: 9.78 us -> 3.43 us  [call(): pl.pallas_call(kernel, name=name, grid=(1,), in_specs=specs, out_specs=[p...]
  transfers between devices with their start and end apart: 64 -> 59, of which waited for: 33 -> 27; matrix products, arithmetic and copies ran while one was open for 15% -> 18% of each run, Pallas kernels for 7% -> 24%
where the time goes in v2:
time: 349 us; the launch traced here: 342 us
  waiting for transfers between devices  105 us (30%)
  Pallas kernels  93.3 us (27%)
  starting transfers between devices  56.8 us (16%)
  local copies, waits for them, and re-layouts  38 us (11%)
  other arithmetic  34.3 us (10%)
  between operations  15.2 us (4%)
    ppermute x58, waiting for transfers between devices, flip(): return lax.ppermute(value, axis, [(i, i ^ bit) for i in range(size)])  105 us
    pallas_call x17, Pallas kernels, call(): pl.pallas_call(kernel, name=name, grid=(1,), in_specs=specs, out_specs=[p...  93.3 us
    ppermute x58, starting transfers between devices, flip(): return lax.ppermute(value, axis, [(i, i ^ bit) for i in range(size)])  56.7 us
    unnamed x105, local copies, waits for them, and re-layouts  12.6 us
  transfers between devices with their start and end apart: 59, of which 27 were waited for; matrix products, arithmetic and copies ran while one was open for 18% of the time, Pallas kernels for 24%

profile of v2, /device:TPU:0, one launch (start us, length us, event | category | flops | bytes accessed | tf_op | source)
XLA Modules:
  0.0 342.4 jit_solution(6552817132900651718)
XLA Ops:
  11.3 5.5 %front.1 = (bf16[256,512]{1,0:T(8,128)(2,1)}, bf16[256,512]{1,0:T(8,128)(2,1)}, bf16[256,512]{1,0:T(8,128)(2,1)}, bf16[256,512]{1,0:T(8,128)(2,1)}, bf16[256,512...) custom-call(s32[6]{0:T(128)} %stack.55.meta, ...), custom_call_target="tpu_custom_call" | custom-call | flops 805306368 | bytes 8026168 | tf_op jit(solution)/shard_map/front/pallas_call | solution.py:580
  23.7 6.0 %feed.1 = (bf16[256,2048]{1,0:T(8,128)(2,1)}, f32[256,2048]{1,0:T(8,128)}, f32[256,512]{1,0:T(8,128)}) custom-call(bf16[256,512]{1,0:T(8,128)(2,1)} %get-tuple-element.141.second, bf16[2,512,2048]{2,1,0:T(8,128)(2,1)} %iw.5, bf16[2,1,2048]{2,1,0:T(2,128)(2,1)} %copy.94.ib, bf16[2,2048,512]{2,1,0:T(8,128)(2,1)} %dw.5, bf16[2,1,512]{2,1,0:T(2,128)(2,1)} %copy.95.db), custom_call_target="tpu_custom_call" | custom-call | flops 1073741824 | bytes 12331008 | tf_op jit(solution)/shard_map/feed/pallas_call | solution.py:580
  35.1 3.8 %collective-permute-done.2 = f32[2,136,128]{2,1,0:T(8,128)S(1)} collective-permute-done((f32[2,136,128]{2,1,0:T(8,128)S(1)}, f32[2,136,128]{2,1,0:T(8,128)S(1)}, u32[]{:S(2)}, u32[]{:S(2)}) %collective-permute-start.2) | collective-permute-done | bytes 139296 | tf_op jit(solution)/shard_map/ppermute | solution.py:619
  41.7 7.4 %middle.1 = (f32[256,512]{1,0:T(8,128)}, f32[256,512]{1,0:T(8,128)}, bf16[256,512]{1,0:T(8,128)(2,1)}, f32[256,512]{1,0:T(8,128)}, bf16[256,512]{1,0:T(8,128)(2,...) custom-call(s32[6]{0:T(128)} %stack.55.meta, ...), custom_call_target="tpu_custom_call" | custom-call | flops 1073741824 | bytes 12238904 | tf_op jit(solution)/shard_map/middle/pallas_call | solution.py:580
  49.4 5.0 %fusion.36 = (bf16[1,512,2048]{2,1,0:T(8,128)(2,1)}, bf16[1,512,2048]{2,1,0:T(8,128)(2,1)}) fusion(bf16[2,512,2048]{2,1,0:T(8,128)(2,1)} %iw.5), kind=kLoop, calls=%fused_computation.140 | loop fusion | bytes 8388608 | tf_op jit(solution)/shard_map/slice | solution.py:779
  60.0 6.7 %feed_both.1 = (bf16[256,2048]{1,0:T(8,128)(2,1)}, f32[256,512]{1,0:T(8,128)}, bf16[256,2048]{1,0:T(8,128)(2,1)}, f32[256,512]{1,0:T(8,128)}, f32[1,2048]{1,0:T(1,128)}) custom-call(bf16[256,512]{1,0:T(8,128)(2,1)} %get-tuple-element.164.second, bf16[2,512,2048]{2,1,0:T(8,128)(2,1)} %iw.5, bf16[2,1,2048]{2,1,0:T(2,128)(2,1)} %copy.94.ib, ...), custom_call_target="tpu_custom_call" | custom-call | flops 2147483648 | bytes 12077056 | tf_op jit(solution)/shard_map/feed_both/pallas_call | solution.py:580
  73.5 4.1 %collective-permute-done.8 = f32[2,136,128]{2,1,0:T(8,128)S(1)} collective-permute-done((f32[2,136,128]{2,1,0:T(8,128)S(1)}, f32[2,136,128]{2,1,0:T(8,128)S(1)}, u32[]{:S(2)}, u32[]{:S(2)}) %collective-permute-start.8) | collective-permute-done | bytes 139296 | tf_op jit(solution)/shard_map/ppermute | solution.py:619
  80.4 4.8 %turn.1 = (f32[256,512]{1,0:T(8,128)}, f32[256,512]{1,0:T(8,128)}, bf16[256,512]{1,0:T(8,128)(2,1)}, bf16[256,512]{1,0:T(8,128)(2,1)}, bf16[256,512]{1,0:T(8,128...) custom-call(s32[6]{0:T(128)} %stack.55.meta, ...), custom_call_target="tpu_custom_call" | custom-call | flops 402653184 | bytes 6590520 | tf_op jit(solution)/shard_map/turn/pallas_call | solution.py:580
  90.5 4.9 %intra_back.2 = (f32[256,512]{1,0:T(8,128)}, f32[256,512]{1,0:T(8,128)}, f32[256,512]{1,0:T(8,128)}) custom-call(s32[6]{0:T(128)} %stack.55.meta, s32[2,4]{1,0:T(2,128)} %starts.17, bf16[256,512]{1,0:T(8,128)(2,1)} %get-tuple-element.183.fq, bf16[256,512]{1,0:T(8,128)(2,1)} %get-tuple-element.172.fk, bf16[256,512]{1,0:T(8,128)(2,1)} %get-tuple-element.173.v, ...), custom_call_target="tpu_custom_call" | custom-call | flops 536870912 | bytes 3948600 | tf_op jit(solution)/shard_map/intra_back/pallas_call | solution.py:580
  96.1 3.4 collective-permute-start.12
  99.5 4.1 %copy.123 = bf16[1,512,2048]{1,2,0:T(8,128)(2,1)} copy(bf16[1,512,2048]{2,1,0:T(8,128)(2,1)} %get-tuple-element.324) | data formatting | bytes 4194304
  116.5 8.5 %turn_back.1 = (bf16[256,1536]{1,0:T(8,128)(2,1)}, f32[1,1536]{1,0:T(1,128)}, f32[2,512]{1,0:T(2,128)}, f32[2,512]{1,0:T(2,128)}, f32[256,512]{1,0:T(8,128)}, /*...) custom-call(s32[6]{0:T(128)} %stack.55.meta, ...), custom_call_target="tpu_custom_call" | custom-call | flops 1073741824 | bytes 14078008 | tf_op jit(solution)/shard_map/turn_back/pallas_call | solution.py:580
  135.0 4.3 %packed_grad.3 = (f32[2,256,512]{2,1,0:T(8,128)}, f32[2,256,512]{2,1,0:T(8,128)}, f32[2,256,512]{2,1,0:T(8,128)}, f32[2,256,512]{2,1,0:T(8,128)}) custom-call(s32[6]{0:T(128)} %stack.55.meta, bf16[256,512]{1,0:T(8,128)(2,1)} %get-tuple-element.253.first, bf16[256,512]{1,0:T(8,128)(2,1)} %get-tuple-element.254.att_low, ...), custom_call_target="tpu_custom_call" | custom-call | flops 536870912 | bytes 5767192 | tf_op jit(solution)/shard_map/packed_grad/pallas_call | solution.py:580
  139.2 5.5 %feed_back.1 = (bf16[256,2048]{1,0:T(8,128)(2,1)}, f32[256,512]{1,0:T(8,128)}, f32[1,2048]{1,0:T(1,128)}) custom-call(f32[256,2048]{1,0:T(8,128)} %get-tuple-element.205.slope, bf16[256,512]{1,0:T(8,128)(2,1)} %get-tuple-element.207.up, bf16[2,512,2048]{2,1,0:T(8,128)(2,1)} %iw.5, bf16[2,2048,512]{2,1,0:T(8,128)(2,1)} %dw.5), custom_call_target="tpu_custom_call" | custom-call | flops 1073741824 | bytes 12328960 | tf_op jit(solution)/shard_map/feed_back/pallas_call | solution.py:580
  147.7 4.9 %intra_back.3 = (f32[256,512]{1,0:T(8,128)}, f32[256,512]{1,0:T(8,128)}, f32[256,512]{1,0:T(8,128)}) custom-call(s32[6]{0:T(128)} %stack.55.meta, s32[2,4]{1,0:T(2,128)} %starts.17, bf16[256,512]{1,0:T(8,128)(2,1)} %get-tuple-element.211.fq.fq0, bf16[256,512]{1,0:T(8,128)(2,1)} %get-tuple-element.148.fk, bf16[256,512]{1,0:T(8,128)(2,1)} %get-tuple-element.149.v, ...), custom_call_target="tpu_custom_call" | custom-call | flops 536870912 | bytes 3948600 | tf_op jit(solution)/shard_map/intra_back/pallas_call | solution.py:580
  152.6 3.7 %collective-permute-done.18 = f32[2,136,128]{2,1,0:T(8,128)S(1)} collective-permute-done((f32[2,136,128]{2,1,0:T(8,128)S(1)}, f32[2,136,128]{2,1,0:T(8,128)S(1)}, u32[]{:S(2)}, u32[]{:S(2)}) %collective-permute-start.18) | collective-permute-done | bytes 139296 | tf_op jit(solution)/shard_map/ppermute | solution.py:619
  160.2 6.3 %last.1 = (bf16[256,1536]{1,0:T(8,128)(2,1)}, f32[1,1536]{1,0:T(1,128)}, f32[2,512]{1,0:T(2,128)}, f32[2,512]{1,0:T(2,128)}, f32[256,512]{1,0:T(8,128)}) custom-call(s32[6]{0:T(128)} %stack.55.meta, s32[2,4]{1,0:T(2,128)} %starts.17, f32[2,136,128]{2,1,0:T(8,128)} %get-tuple-element.329.mine, f32[2,136,128]{2,1,0:T(8,128)} %copy-done.38, ...), custom_call_target="tpu_custom_call" | custom-call | flops 805306368 | bytes 9865272 | tf_op jit(solution)/shard_map/last/pallas_call | solution.py:580
  168.8 4.4 %packed_grad.2 = (f32[2,256,512]{2,1,0:T(8,128)}, f32[2,256,512]{2,1,0:T(8,128)}, f32[2,256,512]{2,1,0:T(8,128)}, f32[2,256,512]{2,1,0:T(8,128)}) custom-call(s32[6]{0:T(128)} %stack.55.meta, bf16[256,512]{1,0:T(8,128)(2,1)} %get-tuple-element.227.first, bf16[256,512]{1,0:T(8,128)(2,1)} %get-tuple-element.228.att_low, ...), custom_call_target="tpu_custom_call" | custom-call | flops 536870912 | bytes 5767192 | tf_op jit(solution)/shard_map/packed_grad/pallas_call | solution.py:580
  179.0 10.7 %collective-permute-done.47 = f32[256,512]{1,0:T(8,128)S(1)} collective-permute-done((f32[256,512]{1,0:T(8,128)S(1)}, f32[256,512]{1,0:T(8,128)S(1)}, u32[]{:S(2)}, u32[]{:S(2)}) %collective-permute-start.47) | collective-permute-done | bytes 524320 | tf_op jit(solution)/shard_map/ppermute | solution.py:619
  196.9 3.9 %collective-permute-done.48 = f32[128,512]{1,0:T(8,128)S(1)} collective-permute-done((f32[128,512]{1,0:T(8,128)S(1)}, f32[128,512]{1,0:T(8,128)S(1)}, u32[]{:S(2)}, u32[]{:S(2)}) %collective-permute-start.48) | collective-permute-done | bytes 262176 | tf_op jit(solution)/shard_map/ppermute | solution.py:619
  201.6 3.7 %collective-permute-done.54 = f32[128,512]{1,0:T(8,128)S(1)} collective-permute-done((f32[128,512]{1,0:T(8,128)S(1)}, f32[128,512]{1,0:T(8,128)S(1)}, u32[]{:S(2)}, u32[]{:S(2)}) %collective-permute-start.54) | collective-permute-done | bytes 262176 | tf_op jit(solution)/shard_map/ppermute | solution.py:619
  208.5 5.9 %collective-permute-done.49 = f32[64,512]{1,0:T(8,128)S(1)} collective-permute-done((f32[64,512]{1,0:T(8,128)S(1)}, f32[64,512]{1,0:T(8,128)S(1)}, u32[]{:S(2)}, u32[]{:S(2)}) %collective-permute-start.49) | collective-permute-done | bytes 131104 | tf_op jit(solution)/shard_map/ppermute | solution.py:619
  219.6 7.5 %feed_grad.2 = (f32[512,512]{1,0:T(8,128)}, f32[512,512]{1,0:T(8,128)}) custom-call(s32[6]{0:T(128)} %stack.55.meta, f32[4,2,256,512]{3,2,1,0:T(8,128)} %bitcast.106, f32[128,512]{1,0:T(8,128)} %get-tuple-element.202.refs_1_, f32[128,512]{1,0:T(8,128)} %get-tuple-element.204.refs_2_, f32[128,512]{1,0:T(8,128)} %copy-done.34, f32[256,512]{1,0:T(8,128)} %copy-done.48, ...), custom_call_target="tpu_custom_call" | custom-call | flops 2147483648 | bytes 9438232 | tf_op jit(solution)/shard_map/feed_grad/pallas_call | solution.py:580
  228.2 7.3 %feed_grad.3 = (f32[512,512]{1,0:T(8,128)}, f32[512,512]{1,0:T(8,128)}) custom-call(s32[6]{0:T(128)} %stack.55.meta, f32[4,2,256,512]{3,2,1,0:T(8,128)} %bitcast.107, f32[128,512]{1,0:T(8,128)} %get-tuple-element.160.refs_1_, f32[128,512]{1,0:T(8,128)} %get-tuple-element.162.refs_2_, f32[128,512]{1,0:T(8,128)} %copy-done.30, ...), custom_call_target="tpu_custom_call" | custom-call | flops 2147483648 | bytes 9438232 | tf_op jit(solution)/shard_map/feed_grad/pallas_call | solution.py:580
  241.9 4.8 %collective-permute-done.35 = f32[128,512]{1,0:T(8,128)S(1)} collective-permute-done((f32[128,512]{1,0:T(8,128)S(1)}, f32[128,512]{1,0:T(8,128)S(1)}, u32[]{:S(2)}, u32[]{:S(2)}) %collective-permute-start.35) | collective-permute-done | bytes 262176 | tf_op jit(solution)/shard_map/ppermute | solution.py:619
  257.6 11.9 %collective-permute-done.23 = f32[72,512]{1,0:T(8,128)S(1)} collective-permute-done((f32[72,512]{1,0:T(8,128)S(1)}, f32[72,512]{1,0:T(8,128)S(1)}, u32[]{:S(2)}, u32[]{:S(2)}) %collective-permute-start.23) | collective-permute-done | bytes 147488 | tf_op jit(solution)/shard_map/ppermute | solution.py:619
  272.6 9.1 %collective-permute-done.42 = f32[256,512]{1,0:T(8,128)S(1)} collective-permute-done((f32[256,512]{1,0:T(8,128)S(1)}, f32[256,512]{1,0:T(8,128)S(1)}, u32[]{:S(2)}, u32[]{:S(2)}) %collective-permute-start.42) | collective-permute-done | bytes 524320 | tf_op jit(solution)/shard_map/ppermute | solution.py:619
  289.8 10.4 %collective-permute-done.30 = f32[128,512]{1,0:T(8,128)S(1)} collective-permute-done((f32[128,512]{1,0:T(8,128)S(1)}, f32[128,512]{1,0:T(8,128)S(1)}, u32[]{:S(2)}, u32[]{:S(2)}) %collective-permute-start.30) | collective-permute-done | bytes 262176 | tf_op jit(solution)/shard_map/ppermute | solution.py:619
  301.6 4.1 %collective-permute-done.43 = f32[128,512]{1,0:T(8,128)S(1)} collective-permute-done((f32[128,512]{1,0:T(8,128)S(1)}, f32[128,512]{1,0:T(8,128)S(1)}, u32[]{:S(2)}, u32[]{:S(2)}) %collective-permute-start.43) | collective-permute-done | bytes 262176 | tf_op jit(solution)/shard_map/ppermute | solution.py:619
  310.4 4.6 %collective-permute-done.44.refs_8_ = f32[128,512]{1,0:T(8,128)S(1)} collective-permute-done((f32[128,512]{1,0:T(8,128)S(1)}, f32[128,512]{1,0:T(8,128)S(1)}, u32[]{:S(2)}, u32[]{:S(2)}) %collective-permute-start.44) | collective-permute-done | bytes 262176 | tf_op jit(solution)/shard_map/ppermute | solution.py:619
  321.2 7.4 %collective-permute-done.32.refs_2_ = f32[256,512]{1,0:T(8,128)S(1)} collective-permute-done((f32[256,512]{1,0:T(8,128)S(1)}, f32[256,512]{1,0:T(8,128)S(1)}, u32[]{:S(2)}, u32[]{:S(2)}) %collective-permute-start.32) | collective-permute-done | bytes 524320 | tf_op jit(solution)/shard_map/ppermute | solution.py:619
  330.7 4.0 %join.1 = (f32[2,64,2048]{2,1,0:T(8,128)}, f32[2,256,512]{2,1,0:T(8,128)}, f32[2,64,1536]{2,1,0:T(8,128)}, f32[2,64,512]{2,1,0:T(8,128)}) custom-call(s32[6]{0:T(128)} %stack.55.meta, f32[128,512]{1,0:T(8,128)} %copy-done.2, f32[128,512]{1,0:T(8,128)} %copy-done.12, f32[256,512]{1,0:T(8,128)} %copy-done.24, f32[72,512]{1,0:T(8,128)} %copy-done.14, ...), custom_call_target="tpu_custom_call" | custom-call | flops 134217728 | bytes 6324248 | tf_op jit(solution)/shard_map/join/pallas_call | solution.py:580
  (341 shorter events, 138.6 us)
Async XLA Ops:
  7.2 212.5 %all-gather.3.cloned.1.call-start = ((), (), s32[]{:S(2)}) async-start(), calls=%async_computation | async-start | bytes 5242880 | tf_op jit(solution)/shard_map/all_gather | solution.py:824
  54.5 13.2 %collective-permute-start.6 = (f32[128,512]{1,0:T(8,128)S(1)}, f32[128,512]{1,0:T(8,128)S(1)}, u32[]{:S(2)}, u32[]{:S(2)}) collective-permute-start(f32[128,512]{1,0:T(8,128)S(1)} %copy-done.28), channel_id=1, source_target_pairs={{0,8},{8,0},{16,24},{24,16},{1,9},{9,1},{17,25},{25,17},{2,10},{10... | collective-permute-start | bytes 786440 | tf_op jit(solution)/shard_map/ppermute | solution.py:619
  114.9 112.2 %collective-permute-start.39 = (f32[256,512]{1,0:T(8,128)}, f32[256,512]{1,0:T(8,128)}, u32[]{:S(2)}, u32[]{:S(2)}) collective-permute-start(f32[256,512]{1,0:T(8,128)} %pad_maximum_fusion.5), channel_id=1, source_target_pairs={{0,16},{8,24},{16,0},{24,8},{1,17},{9,25},{17,1},{25,9},{2,18},{10... | collective-permute-start | bytes 1572872 | tf_op jit(solution)/shard_map/ppermute | solution.py:619
  126.2 102.0 %collective-permute-start.40 = (f32[256,512]{1,0:T(8,128)}, f32[256,512]{1,0:T(8,128)}, u32[]{:S(2)}, u32[]{:S(2)}) collective-permute-start(f32[256,512]{1,0:T(8,128)} %pad_maximum_fusion.6), channel_id=1, source_target_pairs={{0,8},{8,0},{16,24},{24,16},{1,9},{9,1},{17,25},{25,17},{2,10},{10... | collective-permute-start | bytes 1572872 | tf_op jit(solution)/shard_map/ppermute | solution.py:619
  132.8 13.3 %collective-permute-start.16 = (f32[128,512]{1,0:T(8,128)}, f32[128,512]{1,0:T(8,128)S(1)}, u32[]{:S(2)}, u32[]{:S(2)}) collective-permute-start(f32[128,512]{1,0:T(8,128)} %get-tuple-element.202.refs_1_), channel_id=1, source_target_pairs={{0,8},{8,0},{16,24},{24,16},{1,9},{9,1},{17,25},{25,17},{2,10},{10... | collective-permute-start | bytes 786440 | tf_op jit(solution)/shard_map/ppermute | solution.py:619
  144.8 29.7 %collective-permute-start.46 = (f32[2,256,512]{2,1,0:T(8,128)}, f32[2,256,512]{2,1,0:T(8,128)}, u32[]{:S(2)}, u32[]{:S(2)}) collective-permute-start(f32[2,256,512]{2,1,0:T(8,128)} %get-tuple-element.257), channel_id=1, source_target_pairs={{0,1},{1,0},{2,3},{3,2},{4,5},{5,4},{6,7},{7,6},{8,9},{9,8},{10,11... | collective-permute-start | bytes 3145736 | tf_op jit(solution)/shard_map/ppermute | solution.py:619
  146.1 30.6 %collective-permute-start.52 = (f32[2,256,512]{2,1,0:T(8,128)}, f32[2,256,512]{2,1,0:T(8,128)}, u32[]{:S(2)}, u32[]{:S(2)}) collective-permute-start(f32[2,256,512]{2,1,0:T(8,128)} %get-tuple-element.259), channel_id=1, source_target_pairs={{0,1},{1,0},{2,3},{3,2},{4,5},{5,4},{6,7},{7,6},{8,9},{9,8},{10,11... | collective-permute-start | bytes 3145736 | tf_op jit(solution)/shard_map/ppermute | solution.py:619
  173.1 19.8 %collective-permute-start.33 = (f32[2,256,512]{2,1,0:T(8,128)}, f32[2,256,512]{2,1,0:T(8,128)}, u32[]{:S(2)}, u32[]{:S(2)}) collective-permute-start(f32[2,256,512]{2,1,0:T(8,128)} %get-tuple-element.248), channel_id=1, source_target_pairs={{0,1},{1,0},{2,3},{3,2},{4,5},{5,4},{6,7},{7,6},{8,9},{9,8},{10,11... | collective-permute-start | bytes 3145736 | tf_op jit(solution)/shard_map/ppermute | solution.py:619
  175.8 13.9 %collective-permute-start.47 = (f32[256,512]{1,0:T(8,128)S(1)}, f32[256,512]{1,0:T(8,128)S(1)}, u32[]{:S(2)}, u32[]{:S(2)}) collective-permute-start(f32[256,512]{1,0:T(8,128)S(1)} %fusion.7), channel_id=1, source_target_pairs={{0,8},{8,0},{16,24},{24,16},{1,9},{9,1},{17,25},{25,17},{2,10},{10... | collective-permute-start | bytes 1572872 | tf_op jit(solution)/shard_map/ppermute | solution.py:619
  178.0 13.7 %collective-permute-start.53 = (f32[256,512]{1,0:T(8,128)S(1)}, f32[256,512]{1,0:T(8,128)S(1)}, u32[]{:S(2)}, u32[]{:S(2)}) collective-permute-start(f32[256,512]{1,0:T(8,128)S(1)} %fusion.4), channel_id=1, source_target_pairs={{0,16},{8,24},{16,0},{24,8},{1,17},{9,25},{17,1},{25,9},{2,18},{10... | collective-permute-start | bytes 1572872 | tf_op jit(solution)/shard_map/ppermute | solution.py:619
  189.7 17.3 %collective-permute-start.20 = (f32[2,288,512]{2,1,0:T(8,128)S(1)}, f32[2,288,512]{2,1,0:T(8,128)S(1)}, u32[]{:S(2)}, u32[]{:S(2)}) collective-permute-start(f32[2,288,512]{2,1,0:T(8,128)S(1)} %bitcast.94), channel_id=1, source_target_pairs={{0,1},{1,0},{2,3},{3,2},{4,5},{5,4},{6,7},{7,6},{8,9},{9,8},{10,11... | collective-permute-start | bytes 3538952 | tf_op jit(solution)/shard_map/ppermute | solution.py:619
  200.9 15.4 %collective-permute-start.26 = (f32[256,512]{1,0:T(8,128)S(1)}, f32[256,512]{1,0:T(8,128)S(1)}, u32[]{:S(2)}, u32[]{:S(2)}) collective-permute-start(f32[256,512]{1,0:T(8,128)S(1)} %copy-done.23), channel_id=1, source_target_pairs={{0,16},{8,24},{16,0},{24,8},{1,17},{9,25},{17,1},{25,9},{2,18},{10... | collective-permute-start | bytes 1572872 | tf_op jit(solution)/shard_map/ppermute | solution.py:619
  205.3 12.8 %collective-permute-start.27 = (f32[256,512]{1,0:T(8,128)S(1)}, f32[256,512]{1,0:T(8,128)S(1)}, u32[]{:S(2)}, u32[]{:S(2)}) collective-permute-start(f32[256,512]{1,0:T(8,128)S(1)} %copy-done.22), channel_id=1, source_target_pairs={{0,8},{8,0},{16,24},{24,16},{1,9},{9,1},{17,25},{25,17},{2,10},{10... | collective-permute-start | bytes 1572872 | tf_op jit(solution)/shard_map/ppermute | solution.py:619
  214.4 21.1 %collective-permute-start.34 = (f32[256,512]{1,0:T(8,128)}, f32[256,512]{1,0:T(8,128)}, u32[]{:S(2)}, u32[]{:S(2)}) collective-permute-start(f32[256,512]{1,0:T(8,128)} %fusion.10), channel_id=1, source_target_pairs={{0,16},{8,24},{16,0},{24,8},{1,17},{9,25},{17,1},{25,9},{2,18},{10... | collective-permute-start | bytes 1572872 | tf_op jit(solution)/shard_map/ppermute | solution.py:619
  216.3 23.2 %collective-permute-start.55 = (f32[64,512]{1,0:T(8,128)}, f32[64,512]{1,0:T(8,128)}, u32[]{:S(2)}, u32[]{:S(2)}) collective-permute-start(f32[64,512]{1,0:T(8,128)} %slice.268), channel_id=1, source_target_pairs={{0,4},{1,5},{2,6},{3,7},{4,0},{5,1},{6,2},{7,3},{8,12},{9,13},{10,... | collective-permute-start | bytes 393224 | tf_op jit(solution)/shard_map/ppermute | solution.py:619
  218.9 18.6 %collective-permute-start.21 = (f32[288,512]{1,0:T(8,128)}, f32[288,512]{1,0:T(8,128)}, u32[]{:S(2)}, u32[]{:S(2)}) collective-permute-start(f32[288,512]{1,0:T(8,128)} %fusion.1), channel_id=1, source_target_pairs={{0,8},{8,0},{16,24},{24,16},{1,9},{9,1},{17,25},{25,17},{2,10},{10... | collective-permute-start | bytes 1769480 | tf_op jit(solution)/shard_map/ppermute | solution.py:619
  227.1 55.2 %collective-permute-start.50 = (f32[64,512]{1,0:T(8,128)}, f32[64,512]{1,0:T(8,128)}, u32[]{:S(2)}, u32[]{:S(2)}) collective-permute-start(f32[64,512]{1,0:T(8,128)} %slice_add_fusion.16), channel_id=1, source_target_pairs={{0,16},{8,24},{16,0},{24,8},{1,17},{9,25},{17,1},{25,9},{2,18},{10... | collective-permute-start | bytes 393224 | tf_op jit(solution)/shard_map/ppermute | solution.py:619
  228.2 20.4 %collective-permute-start.28 = (f32[512,512]{1,0:T(8,128)}, f32[512,512]{1,0:T(8,128)}, u32[]{:S(2)}, u32[]{:S(2)}) collective-permute-start(f32[512,512]{1,0:T(8,128)} %get-tuple-element.246), channel_id=1, source_target_pairs={{0,1},{1,0},{2,3},{3,2},{4,5},{5,4},{6,7},{7,6},{8,9},{9,8},{10,11... | collective-permute-start | bytes 3145736 | tf_op jit(solution)/shard_map/ppermute | solution.py:619
  235.5 18.6 %collective-permute-start.41 = (f32[512,512]{1,0:T(8,128)}, f32[512,512]{1,0:T(8,128)S(1)}, u32[]{:S(2)}, u32[]{:S(2)}) collective-permute-start(f32[512,512]{1,0:T(8,128)} %get-tuple-element.252), channel_id=1, source_target_pairs={{0,1},{1,0},{2,3},{3,2},{4,5},{5,4},{6,7},{7,6},{8,9},{9,8},{10,11... | collective-permute-start | bytes 3145736 | tf_op jit(solution)/shard_map/ppermute | solution.py:619
  239.6 14.4 %collective-permute-start.22 = (f32[144,512]{1,0:T(8,128)S(1)}, f32[144,512]{1,0:T(8,128)S(1)}, u32[]{:S(2)}, u32[]{:S(2)}) collective-permute-start(f32[144,512]{1,0:T(8,128)S(1)} %slice.236), channel_id=1, source_target_pairs={{0,2},{1,3},{2,0},{3,1},{4,6},{5,7},{6,4},{7,5},{8,10},{9,11},{10,... | collective-permute-start | bytes 884744 | tf_op jit(solution)/shard_map/ppermute | solution.py:619
  246.8 39.0 %collective-permute-start.56 = (f32[64,512]{1,0:T(8,128)S(1)}, f32[64,512]{1,0:T(8,128)S(1)}, u32[]{:S(2)}, u32[]{:S(2)}) collective-permute-start(f32[64,512]{1,0:T(8,128)S(1)} %slice_add_fusion.15), channel_id=1, source_target_pairs={{0,8},{8,0},{16,24},{24,16},{1,9},{9,1},{17,25},{25,17},{2,10},{10... | collective-permute-start | bytes 393224 | tf_op jit(solution)/shard_map/ppermute | solution.py:619
  254.0 17.6 %collective-permute-start.29 = (f32[256,512]{1,0:T(8,128)S(1)}, f32[256,512]{1,0:T(8,128)S(1)}, u32[]{:S(2)}, u32[]{:S(2)}) collective-permute-start(f32[256,512]{1,0:T(8,128)S(1)} %slice.244), channel_id=1, source_target_pairs={{0,2},{1,3},{2,0},{3,1},{4,6},{5,7},{6,4},{7,5},{8,10},{9,11},{10,... | collective-permute-start | bytes 1572872 | tf_op jit(solution)/shard_map/ppermute | solution.py:619
  254.1 15.5 %collective-permute-start.23 = (f32[72,512]{1,0:T(8,128)S(1)}, f32[72,512]{1,0:T(8,128)S(1)}, u32[]{:S(2)}, u32[]{:S(2)}) collective-permute-start(f32[72,512]{1,0:T(8,128)S(1)} %slice.238), channel_id=1, source_target_pairs={{0,4},{1,5},{2,6},{3,7},{4,0},{5,1},{6,2},{7,3},{8,12},{9,13},{10,... | collective-permute-start | bytes 442376 | tf_op jit(solution)/shard_map/ppermute | solution.py:619
  257.2 24.5 %collective-permute-start.42 = (f32[256,512]{1,0:T(8,128)S(1)}, f32[256,512]{1,0:T(8,128)S(1)}, u32[]{:S(2)}, u32[]{:S(2)}) collective-permute-start(f32[256,512]{1,0:T(8,128)S(1)} %slice.254), channel_id=1, source_target_pairs={{0,2},{1,3},{2,0},{3,1},{4,6},{5,7},{6,4},{7,5},{8,10},{9,11},{10,... | collective-permute-start | bytes 1572872 | tf_op jit(solution)/shard_map/ppermute | solution.py:619
  269.5 18.1 %collective-permute-start.37 = (f32[64,512]{1,0:T(8,128)S(1)}, f32[64,512]{1,0:T(8,128)S(1)}, u32[]{:S(2)}, u32[]{:S(2)}) collective-permute-start(f32[64,512]{1,0:T(8,128)S(1)} %slice_add_fusion.17), channel_id=1, source_target_pairs={{0,8},{8,0},{16,24},{24,16},{1,9},{9,1},{17,25},{25,17},{2,10},{10... | collective-permute-start | bytes 393224 | tf_op jit(solution)/shard_map/ppermute | solution.py:619
  271.6 16.6 %collective-permute-start.24 = (f32[72,512]{1,0:T(8,128)S(1)}, f32[72,512]{1,0:T(8,128)S(1)}, u32[]{:S(2)}, u32[]{:S(2)}) collective-permute-start(f32[72,512]{1,0:T(8,128)S(1)} %slice_add_fusion.14), channel_id=1, source_target_pairs={{0,16},{8,24},{16,0},{24,8},{1,17},{9,25},{17,1},{25,9},{2,18},{10... | collective-permute-start | bytes 442376 | tf_op jit(solution)/shard_map/ppermute | solution.py:619
  281.7 18.5 %collective-permute-start.30 = (f32[128,512]{1,0:T(8,128)S(1)}, f32[128,512]{1,0:T(8,128)S(1)}, u32[]{:S(2)}, u32[]{:S(2)}) collective-permute-start(f32[128,512]{1,0:T(8,128)S(1)} %slice.246), channel_id=1, source_target_pairs={{0,4},{1,5},{2,6},{3,7},{4,0},{5,1},{6,2},{7,3},{8,12},{9,13},{10,... | collective-permute-start | bytes 786440 | tf_op jit(solution)/shard_map/ppermute | solution.py:619
  282.4 23.4 %collective-permute-start.43 = (f32[128,512]{1,0:T(8,128)S(1)}, f32[128,512]{1,0:T(8,128)S(1)}, u32[]{:S(2)}, u32[]{:S(2)}) collective-permute-start(f32[128,512]{1,0:T(8,128)S(1)} %slice.256), channel_id=1, source_target_pairs={{0,4},{1,5},{2,6},{3,7},{4,0},{5,1},{6,2},{7,3},{8,12},{9,13},{10,... | collective-permute-start | bytes 786440 | tf_op jit(solution)/shard_map/ppermute | solution.py:619
  285.8 35.5 %collective-permute-start.51 = (f32[64,512]{1,0:T(8,128)S(1)}, f32[64,512]{1,0:T(8,128)}, u32[]{:S(2)}, u32[]{:S(2)}) collective-permute-start(f32[64,512]{1,0:T(8,128)S(1)} %add.355.refs_10_), channel_id=1, source_target_pairs={{0,8},{8,0},{16,24},{24,16},{1,9},{9,1},{17,25},{25,17},{2,10},{10... | collective-permute-start | bytes 393224 | tf_op jit(solution)/shard_map/ppermute | solution.py:619
  287.6 33.6 %collective-permute-start.57 = (f32[64,512]{1,0:T(8,128)S(1)}, f32[64,512]{1,0:T(8,128)}, u32[]{:S(2)}, u32[]{:S(2)}) collective-permute-start(f32[64,512]{1,0:T(8,128)S(1)} %add.363.refs_12_), channel_id=1, source_target_pairs={{0,16},{8,24},{16,0},{24,8},{1,17},{9,25},{17,1},{25,9},{2,18},{10... | collective-permute-start | bytes 393224 | tf_op jit(solution)/shard_map/ppermute | solution.py:619
  288.2 33.0 %collective-permute-start.38 = (f32[64,512]{1,0:T(8,128)S(1)}, f32[64,512]{1,0:T(8,128)}, u32[]{:S(2)}, u32[]{:S(2)}) collective-permute-start(f32[64,512]{1,0:T(8,128)S(1)} %add.344.refs_5_), channel_id=1, source_target_pairs={{0,16},{8,24},{16,0},{24,8},{1,17},{9,25},{17,1},{25,9},{2,18},{10... | collective-permute-start | bytes 393224 | tf_op jit(solution)/shard_map/ppermute | solution.py:619
  315.0 13.6 %collective-permute-start.32 = (f32[256,512]{1,0:T(8,128)S(1)}, f32[256,512]{1,0:T(8,128)S(1)}, u32[]{:S(2)}, u32[]{:S(2)}) collective-permute-start(f32[256,512]{1,0:T(8,128)S(1)} %pad_maximum_fusion.4), channel_id=1, source_target_pairs={{0,8},{8,0},{16,24},{24,16},{1,9},{9,1},{17,25},{25,17},{2,10},{10... | collective-permute-start | bytes 1572872 | tf_op jit(solution)/shard_map/ppermute | solution.py:619
  (77 other events, 846.1 us)
Sparse Core Ops, SparseCore 0:
  39.9 58.2 all-gather.2
